TPU v7x, 256 devices: a whole 4x4x8 slice. The times are simulated.
256 devices in a mesh: replica: 16 (over z_hi, x), tensor: 16 (over z_lo, y, core).
Axes of the slice: x: 4, y: 4, z: 8 (z_hi: 4, z_lo: 2; z = z_hi * 2 + z_lo), core: 2. Of those that a mesh axis runs over, the one named last changes fastest.
Arguments:
- tokens: bfloat16 [16, 384, 2048], P('replica', 'tensor'), may hold values from -6 to 6
- targets: bfloat16 [16, 384, 2048], P('replica', 'tensor'), may hold values from -6 to 6
- gate_weight: bfloat16 [16, 2048, 7168], P('replica', None, 'tensor'), may hold values from -6 to 6
- probes: bfloat16 [16, 2048, 7168], P('replica', None, 'tensor'), may hold values from -6 to 6
- tracker: bfloat16 [16, 2048, 7168], P('replica', None, 'tensor'), may hold values from 0.049804688 to 2
- up_weight: bfloat16 [2048, 7168], P('replica', 'tensor'), may hold values from -6 to 6
- down_weight: bfloat16 [7168, 2048], P('tensor', 'replica'), may hold values from -6 to 6
- neighbours: int32 [16, 6], replicated, may hold values from 0 to 15, as said below
- numerators: int32 [16, 6], replicated, may hold values from 0 to 8, as said below
Outputs:
- mixed_weights: bfloat16 [16, 2048, 7168], P('replica', None, 'tensor')
- mixed_tracker: bfloat16 [16, 2048, 7168], P('replica', None, 'tensor')
Inputs may be any that keep to these rules, and one draw needn't show every extreme that they name: `neighbours`: every slot of row r holds r itself or a replica r - o modulo 16 with o one of 1, -1, 2, -2, 4, -4, each o at most once in a row; a row has between 2 and 6 slots that are not r, and some row has 6. `numerators`: A numerator is 0 exactly in slots that hold the row's own replica, and 4 to 8 elsewhere.
All inputs are finite; a program needn't handle non-finite values.
Results may differ from a plain program's by a relative error of at most 0.0058.
Values may be sent and summed in bfloat16 or wider, within the bound.
A program may use at most 128 MiB of HBM per device.

v0:
```python
import math

import jax
import jax.numpy as jnp
from jax import lax
from jax.sharding import PartitionSpec as P

D = 2048
FF = 7168
DEN = 64


step_size = 0.1
floor_value = 0.1
tracker_decay = 0.75


def passed_along(value, axis, steps):
    count = lax.axis_size(axis)
    pairs = [(source, (source + steps) % count) for source in range(count)]
    return lax.ppermute(value, axis, pairs)


def mix_shard(shard_value, lag_of_slot, row_numer, self_weight):
    replicas_count = lax.axis_size("replica")
    mixed_sum = self_weight * shard_value.astype(jnp.float32)
    offset_list = [1, -1, 2, -2, 4]
    offset_list = offset_list + [-4]
    for offset_value in offset_list:
        received = passed_along(shard_value, "replica", offset_value)
        matched = jnp.where(lag_of_slot == offset_value % replicas_count, row_numer, 0)
        mixed_sum = mixed_sum + jnp.sum(matched).astype(jnp.float32) / DEN * received.astype(
            jnp.float32
        )
    return mixed_sum.astype(jnp.bfloat16)


def local(
    tokens, targets, gate_weight, probes, tracker, up_weight, down_weight, neighbours, numerators
):
    inv_width = 1.0 / math.sqrt(D)
    inv_hidden = 1.0 / math.sqrt(FF)
    gathered = lax.all_gather(tokens[0], "tensor", axis=0, tiled=True)
    weight_now = gate_weight[0]
    tracker_now = tracker[0]
    probe_here = probes[0]
    gate_pre = jnp.dot(gathered, weight_now, preferred_element_type=jnp.float32) * inv_width
    up_pre = (
        jnp.dot(
            gathered,
            lax.all_gather(up_weight, "replica", axis=0, tiled=True),
            preferred_element_type=jnp.float32,
        )
        * inv_width
    )
    down_full = lax.all_gather(down_weight, "replica", axis=1, tiled=True)
    logistic = jax.nn.sigmoid(gate_pre)
    activated = gate_pre * logistic
    slope_one = logistic * (1.0 + gate_pre * (1.0 - logistic))
    slope_two = logistic * (1.0 - logistic) * (2.0 + gate_pre * (1.0 - 2.0 * logistic))
    hidden = (activated * up_pre).astype(jnp.bfloat16)

    def forward_term(source):
        return jnp.dot(source, down_full, preferred_element_type=jnp.float32) * inv_hidden

    def backward_rows(shard_piece):
        return (
            lax.dot_general(
                shard_piece, down_full, (((1,), (1,)), ((), ())), preferred_element_type=jnp.float32
            )
            * inv_hidden
        )

    outputs = lax.psum_scatter(forward_term(hidden), "tensor", scatter_dimension=0, tiled=True)
    residual = (outputs - targets[0].astype(jnp.float32)).astype(jnp.bfloat16)
    grad_hidden = backward_rows(lax.all_gather(residual, "tensor", axis=0, tiled=True))
    grad_gate = (grad_hidden * up_pre * slope_one).astype(jnp.bfloat16)
    gradient = (
        lax.dot_general(
            gathered, grad_gate, (((0,), (0,)), ((), ())), preferred_element_type=jnp.float32
        )
        * inv_width
    )
    ratio = gradient / jnp.maximum(tracker_now.astype(jnp.float32), floor_value)
    stepped = (weight_now.astype(jnp.float32) - step_size * jnp.clip(ratio, -1.0, 1.0)).astype(
        jnp.bfloat16
    )
    replica_index = lax.axis_index("replica")
    row_links = neighbours[replica_index]
    row_numer = numerators[replica_index]
    lag_of_slot = jnp.mod(replica_index - row_links, lax.axis_size("replica"))
    self_weight = (DEN - jnp.sum(row_numer)).astype(jnp.float32) / DEN
    mixed_weights = mix_shard(stepped, lag_of_slot, row_numer, self_weight)
    probe_pre = jnp.dot(gathered, probe_here, preferred_element_type=jnp.float32) * inv_width
    tangent_hidden = (slope_one * probe_pre * up_pre).astype(jnp.bfloat16)
    tangent_out = lax.psum_scatter(
        forward_term(tangent_hidden), "tensor", scatter_dimension=0, tiled=True
    )
    tangent_res = tangent_out.astype(jnp.bfloat16)
    tangent_grad = backward_rows(lax.all_gather(tangent_res, "tensor", axis=0, tiled=True))
    tangent_gate = (
        (tangent_grad * slope_one + grad_hidden * slope_two * probe_pre) * up_pre
    ).astype(jnp.bfloat16)
    curvature_probe = (
        lax.dot_general(
            gathered, tangent_gate, (((0,), (0,)), ((), ())), preferred_element_type=jnp.float32
        )
        * inv_width
    )
    tracked = (
        tracker_decay * tracker_now.astype(jnp.float32)
        + (1.0 - tracker_decay) * probe_here.astype(jnp.float32) * curvature_probe
    ).astype(jnp.bfloat16)
    mixed_tracker = mix_shard(tracked, lag_of_slot, row_numer, self_weight)
    return (mixed_weights[None], mixed_tracker[None])


def solution(mesh):
    return jax.shard_map(
        local,
        mesh=mesh,
        in_specs=(
            P("replica", "tensor", None),
            P("replica", "tensor", None),
            P("replica", None, "tensor"),
            P("replica", None, "tensor"),
            P("replica", None, "tensor"),
            P("replica", "tensor"),
            P("tensor", "replica"),
            P(),
            P(),
        ),
        out_specs=(P("replica", None, "tensor"), P("replica", None, "tensor")),
        check_vma=False,
    )
```

profile of v0, /device:TPU:16, one launch (start us, length us, event | category | flops | bytes accessed | tf_op | source)
XLA Modules:
  0.0 849.8 jit_solution(12883269303572722295)
XLA Ops:
  7.2 0.0 all-gather.15.cloned.1.call-start
  7.2 0.7 all-gather.15.cloned.1.call-update
  7.9 0.0 all-gather.7.cloned.1.call-start
  7.9 0.7 all-gather.7.cloned.1.call-update
  8.6 0.0 all-gather.9.cloned.1.call-start
  8.7 0.7 all-gather.9.cloned.1.call-update
  9.4 0.0 reduce-scatter.3.cloned.1.call-start
  9.4 38.1 %all-gather.15.cloned.1.call-done = bf16[1,384,2048]{2,1,0:T(8,128)(2,1)} async-done(((bf16[1,24,2048]{2,1,0:T(8,128)(2,1)}), bf16[1,384,2048]{2,1,0:T(8,128)(2,1)}) %all-gather.15.cloned.1.call-update) | async-done | bytes 1572880 | tf_op jit(solution)/shard_map/all_gather | solution.py:43
  47.5 3.2 fusion.24
  50.7 60.8 %all-gather.7.cloned.1.call-done = bf16[2048,448]{0,1:T(8,128)(2,1)} async-done(((bf16[128,448]{0,1:T(8,128)(2,1)}), bf16[2048,448]{0,1:T(8,128)(2,1)}) %all-gather.7.cloned.1.call-update) | async-done | bytes 1835024 | tf_op jit(solution)/shard_map/all_gather | solution.py:51
  111.5 0.0 copy-done.9
  111.5 2.6 fusion.21
  114.1 58.0 %all-gather.9.cloned.1.call-done = bf16[448,2048]{1,0:T(8,128)(2,1)} async-done(((bf16[448,128]{1,0:T(8,128)(2,1)}), bf16[448,2048]{1,0:T(8,128)(2,1)}) %all-gather.9.cloned.1.call-update) | async-done | bytes 1835024 | tf_op jit(solution)/shard_map/all_gather | solution.py:56
  172.1 4.2 convolution_multiply_fusion.1
  176.3 0.0 reduce-scatter.3.cloned.1.call-update
  176.3 0.0 reduce-scatter.5.cloned.1.call-start
  176.4 3.2 fusion.29
  179.6 0.0 copy-start.3
  179.6 0.8 copy-done.3
  180.5 2.8 convolution_multiply_fusion
  183.3 0.0 reduce-scatter.5.cloned.1.call-update
  183.3 0.0 all-gather.11.cloned.1.call-start
  183.4 51.0 %reduce-scatter.3.cloned.1.call-done = f32[24,2048]{1,0:T(8,128)} async-done(((f32[384,2048]{1,0:T(8,128)}), f32[24,2048]{1,0:T(8,128)}) %reduce-scatter.3.cloned.1.call-update) | async-done | bytes 196624 | tf_op jit(solution)/shard_map/reduce_scatter | solution.py:74
  234.4 1.6 fusion.52
  236.0 0.0 all-gather.11.cloned.1.call-update
  236.0 0.0 all-gather.13.cloned.1.call-start
  236.0 66.4 %reduce-scatter.5.cloned.1.call-done = f32[24,2048]{1,0:T(8,128)} async-done(((f32[384,2048]{1,0:T(8,128)}), f32[24,2048]{1,0:T(8,128)}) %reduce-scatter.5.cloned.1.call-update) | async-done | bytes 196624 | tf_op jit(solution)/shard_map/reduce_scatter | solution.py:96
  302.5 1.6 convert_element_type.141
  304.0 0.0 all-gather.13.cloned.1.call-update
  304.1 40.9 %all-gather.11.cloned.1.call-done = bf16[384,2048]{1,0:T(8,128)(2,1)} async-done(((bf16[24,2048]{1,0:T(8,128)(2,1)}), bf16[384,2048]{1,0:T(8,128)(2,1)}) %all-gather.11.cloned.1.call-update) | async-done | bytes 1572880 | tf_op jit(solution)/shard_map/all_gather | solution.py:76
  344.9 2.7 convolution_multiply_fusion.3
  347.6 0.0 copy-done.7
  347.7 0.0 copy-done.8
  347.7 4.7 fusion.8
  352.4 3.8 collective-permute-start.5
  356.2 0.0 collective-permute-start.4
  356.2 6.5 collective-permute-start.3
  362.8 0.0 collective-permute-start.2
  362.8 6.2 collective-permute-start.1
  369.0 128.7 %all-gather.13.cloned.1.call-done = bf16[384,2048]{1,0:T(8,128)(2,1)} async-done(((bf16[24,2048]{1,0:T(8,128)(2,1)}), bf16[384,2048]{1,0:T(8,128)(2,1)}) %all-gather.13.cloned.1.call-update) | async-done | bytes 1572880 | tf_op jit(solution)/shard_map/all_gather | solution.py:100
  497.7 7.2 fusion.7
  504.9 4.9 collective-permute-done.5
  509.8 0.0 collective-permute-start
  509.8 0.0 collective-permute-done.4
  509.8 3.6 collective-permute-start.11
  513.4 128.8 %collective-permute-done.3 = bf16[2048,448]{0,1:T(8,128)(2,1)} collective-permute-done((bf16[2048,448]{0,1:T(8,128)(2,1)}, bf16[2048,448]{0,1:T(8,128)(2,1)}, u32[]{:S(2)}, u32[]{:S(2)}) %collective-permute-start.3) | collective-permute-done | bytes 1835040 | tf_op jit(solution)/shard_map/ppermute | solution.py:21
  642.2 0.5 collective-permute-start.10
  642.7 0.0 collective-permute-done.2
  642.7 7.4 collective-permute-start.9
  650.1 60.0 %collective-permute-done.1 = bf16[2048,448]{0,1:T(8,128)(2,1)} collective-permute-done((bf16[2048,448]{0,1:T(8,128)(2,1)}, bf16[2048,448]{0,1:T(8,128)(2,1)}, u32[]{:S(2)}, u32[]{:S(2)}) %collective-permute-start.1) | collective-permute-done | bytes 1835040 | tf_op jit(solution)/shard_map/ppermute | solution.py:21
  710.1 0.0 collective-permute-start.8
  710.1 0.0 collective-permute-done
  710.1 6.8 collective-permute-start.7
  716.9 33.4 %collective-permute-done.11 = bf16[2048,448]{0,1:T(8,128)(2,1)S(1)} collective-permute-done((bf16[2048,448]{0,1:T(8,128)(2,1)}, bf16[2048,448]{0,1:T(8,128)(2,1)S(1)}, u32[]{:S(2)}, u32[]{:S(2)}) %collective-permute-start.11) | collective-permute-done | bytes 1835040 | tf_op jit(solution)/shard_map/ppermute | solution.py:21
  750.3 0.0 collective-permute-start.6
  750.3 0.8 dynamic-slice_reduce_fusion.1
  751.7 0.8 fusion.53
  756.3 7.2 fusion.13
  763.5 0.0 collective-permute-done.10
  763.5 25.3 %collective-permute-done.9 = bf16[2048,448]{0,1:T(8,128)(2,1)} collective-permute-done((bf16[2048,448]{0,1:T(8,128)(2,1)}, bf16[2048,448]{0,1:T(8,128)(2,1)}, u32[]{:S(2)}, u32[]{:S(2)}) %collective-permute-start.9) | collective-permute-done | bytes 1835040 | tf_op jit(solution)/shard_map/ppermute | solution.py:21
  788.8 0.9 collective-permute-done.8
  789.6 39.1 %collective-permute-done.7 = bf16[2048,448]{0,1:T(8,128)(2,1)} collective-permute-done((bf16[2048,448]{0,1:T(8,128)(2,1)}, bf16[2048,448]{0,1:T(8,128)(2,1)}, u32[]{:S(2)}, u32[]{:S(2)}) %collective-permute-start.7) | collective-permute-done | bytes 1835040 | tf_op jit(solution)/shard_map/ppermute | solution.py:21
  828.8 8.1 collective-permute-done.6
  836.8 6.1 fusion.14
  (17 shorter events, 0.0 us)
Async XLA Ops:
  7.2 40.3 %all-gather.15.cloned.1.call-start = ((), (), s32[]{:S(2)}) async-start(), calls=%async_computation.8 | async-start | bytes 1671168 | tf_op jit(solution)/shard_map/all_gather | solution.py:43
  7.9 103.6 %all-gather.7.cloned.1.call-start = ((), (), s32[]{:S(2)}) async-start(), calls=%async_computation.2 | async-start | bytes 1949696 | tf_op jit(solution)/shard_map/all_gather | solution.py:51
  8.6 163.5 %all-gather.9.cloned.1.call-start = ((), (), s32[]{:S(2)}) async-start(), calls=%async_computation.3 | async-start | bytes 1949696 | tf_op jit(solution)/shard_map/all_gather | solution.py:56
  9.4 225.0 %reduce-scatter.3.cloned.1.call-start = ((), (), s32[]{:S(2)}) async-start(), calls=%async_computation.4 | async-start | bytes 3342336 | tf_op jit(solution)/shard_map/reduce_scatter | solution.py:74
  47.5 64.0 %copy-start.9 = (bf16[1,384,2048]{2,1,0:T(8,128)(2,1)S(1)}, bf16[1,384,2048]{2,1,0:T(8,128)(2,1)}, u32[]{:S(2)}) copy-start(bf16[1,384,2048]{2,1,0:T(8,128)(2,1)} %all-gather.15.cloned.1.call-done) | copy-start | bytes 4718596
  176.3 4.1 copy-start
  176.3 126.1 %reduce-scatter.5.cloned.1.call-start = ((), (), s32[]{:S(2)}) async-start(), calls=%async_computation.6 | async-start | bytes 3342336 | tf_op jit(solution)/shard_map/reduce_scatter | solution.py:96
  179.6 0.8 copy-start.3
  183.3 51.1 %copy-start.4 = (bf16[1,24,2048]{2,1,0:T(8,128)(2,1)S(1)}, bf16[1,24,2048]{2,1,0:T(8,128)(2,1)}, u32[]{:S(2)}) copy-start(bf16[1,24,2048]{2,1,0:T(8,128)(2,1)} %param.10) | copy-start | bytes 294916
  183.3 161.6 %all-gather.11.cloned.1.call-start = ((), (), s32[]{:S(2)}) async-start(), calls=%async_computation.5 | async-start | bytes 1671168 | tf_op jit(solution)/shard_map/all_gather | solution.py:76
  236.0 261.7 %all-gather.13.cloned.1.call-start = ((), (), s32[]{:S(2)}) async-start(), calls=%async_computation.7 | async-start | bytes 1671168 | tf_op jit(solution)/shard_map/all_gather | solution.py:100
  344.9 2.7 copy-start.7
  344.9 2.7 copy-start.8
  347.7 4.7 copy-start.10
  352.4 397.9 %copy-start.5 = (s32[16,6]{0,1:T(8,128)S(1)}, s32[16,6]{0,1:T(8,128)}, u32[]{:S(2)}) copy-start(s32[16,6]{0,1:T(8,128)} %param.17) | copy-start | bytes 1156
  352.4 397.9 %copy-start.6 = (s32[16,6]{0,1:T(8,128)S(1)}, s32[16,6]{0,1:T(8,128)}, u32[]{:S(2)}) copy-start(s32[16,6]{0,1:T(8,128)} %param.16) | copy-start | bytes 1156
  352.4 157.4 %collective-permute-start.5 = (bf16[2048,448]{0,1:T(8,128)(2,1)}, bf16[2048,448]{0,1:T(8,128)(2,1)}, u32[]{:S(2)}, u32[]{:S(2)}) collective-permute-start(bf16[2048,448]{0,1:T(8,128)(2,1)} %fusion.8), channel_id=1, source_target_pairs={{0,192},{16,208},{32,224},{48,240},{64,0},{80,16},{96,32},{112,48}... | collective-permute-start | bytes 5505032 | tf_op jit(solution)/shard_map/ppermute | solution.py:21
  356.2 153.6 %collective-permute-start.4 = (bf16[2048,448]{0,1:T(8,128)(2,1)}, bf16[2048,448]{0,1:T(8,128)(2,1)}, u32[]{:S(2)}, u32[]{:S(2)}) collective-permute-start(bf16[2048,448]{0,1:T(8,128)(2,1)} %fusion.8), channel_id=1, source_target_pairs={{0,64},{16,80},{32,96},{48,112},{64,128},{80,144},{96,160},{112,17... | collective-permute-start | bytes 5505032 | tf_op jit(solution)/shard_map/ppermute | solution.py:21
  356.2 286.0 %collective-permute-start.3 = (bf16[2048,448]{0,1:T(8,128)(2,1)}, bf16[2048,448]{0,1:T(8,128)(2,1)}, u32[]{:S(2)}, u32[]{:S(2)}) collective-permute-start(bf16[2048,448]{0,1:T(8,128)(2,1)} %fusion.8), channel_id=1, source_target_pairs={{0,224},{16,240},{32,0},{48,16},{64,32},{80,48},{96,64},{112,80},{... | collective-permute-start | bytes 5505032 | tf_op jit(solution)/shard_map/ppermute | solution.py:21
  362.8 279.9 %collective-permute-start.2 = (bf16[2048,448]{0,1:T(8,128)(2,1)}, bf16[2048,448]{0,1:T(8,128)(2,1)}, u32[]{:S(2)}, u32[]{:S(2)}) collective-permute-start(bf16[2048,448]{0,1:T(8,128)(2,1)} %fusion.8), channel_id=1, source_target_pairs={{0,32},{16,48},{32,64},{48,80},{64,96},{80,112},{96,128},{112,144}... | collective-permute-start | bytes 5505032 | tf_op jit(solution)/shard_map/ppermute | solution.py:21
  362.8 347.3 %collective-permute-start.1 = (bf16[2048,448]{0,1:T(8,128)(2,1)}, bf16[2048,448]{0,1:T(8,128)(2,1)}, u32[]{:S(2)}, u32[]{:S(2)}) collective-permute-start(bf16[2048,448]{0,1:T(8,128)(2,1)} %fusion.8), channel_id=1, source_target_pairs={{0,240},{16,0},{32,16},{48,32},{64,48},{80,64},{96,80},{112,96},{1... | collective-permute-start | bytes 5505032 | tf_op jit(solution)/shard_map/ppermute | solution.py:21
  509.8 200.3 %collective-permute-start = (bf16[2048,448]{0,1:T(8,128)(2,1)}, bf16[2048,448]{0,1:T(8,128)(2,1)S(1)}, u32[]{:S(2)}, u32[]{:S(2)}) collective-permute-start(bf16[2048,448]{0,1:T(8,128)(2,1)} %fusion.8), channel_id=1, source_target_pairs={{0,16},{16,32},{32,48},{48,64},{64,80},{80,96},{96,112},{112,128},... | collective-permute-start | bytes 5505032 | tf_op jit(solution)/shard_map/ppermute | solution.py:21
  509.8 240.5 %collective-permute-start.11 = (bf16[2048,448]{0,1:T(8,128)(2,1)}, bf16[2048,448]{0,1:T(8,128)(2,1)S(1)}, u32[]{:S(2)}, u32[]{:S(2)}) collective-permute-start(bf16[2048,448]{0,1:T(8,128)(2,1)} %fusion.7), channel_id=1, source_target_pairs={{0,192},{16,208},{32,224},{48,240},{64,0},{80,16},{96,32},{112,48}... | collective-permute-start | bytes 5505032 | tf_op jit(solution)/shard_map/ppermute | solution.py:21
  642.2 121.3 %collective-permute-start.10 = (bf16[2048,448]{0,1:T(8,128)(2,1)}, bf16[2048,448]{0,1:T(8,128)(2,1)}, u32[]{:S(2)}, u32[]{:S(2)}) collective-permute-start(bf16[2048,448]{0,1:T(8,128)(2,1)} %fusion.7), channel_id=1, source_target_pairs={{0,64},{16,80},{32,96},{48,112},{64,128},{80,144},{96,160},{112,17... | collective-permute-start | bytes 5505032 | tf_op jit(solution)/shard_map/ppermute | solution.py:21
  642.7 146.1 %collective-permute-start.9 = (bf16[2048,448]{0,1:T(8,128)(2,1)}, bf16[2048,448]{0,1:T(8,128)(2,1)}, u32[]{:S(2)}, u32[]{:S(2)}) collective-permute-start(bf16[2048,448]{0,1:T(8,128)(2,1)} %fusion.7), channel_id=1, source_target_pairs={{0,224},{16,240},{32,0},{48,16},{64,32},{80,48},{96,64},{112,80},{... | collective-permute-start | bytes 5505032 | tf_op jit(solution)/shard_map/ppermute | solution.py:21
  710.1 79.6 %collective-permute-start.8 = (bf16[2048,448]{0,1:T(8,128)(2,1)}, bf16[2048,448]{0,1:T(8,128)(2,1)}, u32[]{:S(2)}, u32[]{:S(2)}) collective-permute-start(bf16[2048,448]{0,1:T(8,128)(2,1)} %fusion.7), channel_id=1, source_target_pairs={{0,32},{16,48},{32,64},{48,80},{64,96},{80,112},{96,128},{112,144}... | collective-permute-start | bytes 5505032 | tf_op jit(solution)/shard_map/ppermute | solution.py:21
  710.1 40.2 %copy-start.2 = (bf16[2048,448]{0,1:T(8,128)(2,1)}, bf16[2048,448]{0,1:T(8,128)(2,1)S(1)}, u32[]{:S(2)}) copy-start(bf16[2048,448]{0,1:T(8,128)(2,1)S(1)} %collective-permute-done) | copy-start | bytes 5505028
  710.1 118.7 %collective-permute-start.7 = (bf16[2048,448]{0,1:T(8,128)(2,1)}, bf16[2048,448]{0,1:T(8,128)(2,1)}, u32[]{:S(2)}, u32[]{:S(2)}) collective-permute-start(bf16[2048,448]{0,1:T(8,128)(2,1)} %fusion.7), channel_id=1, source_target_pairs={{0,240},{16,0},{32,16},{48,32},{64,48},{80,64},{96,80},{112,96},{1... | collective-permute-start | bytes 5505032 | tf_op jit(solution)/shard_map/ppermute | solution.py:21
  750.3 86.6 %collective-permute-start.6 = (bf16[2048,448]{0,1:T(8,128)(2,1)}, bf16[2048,448]{0,1:T(8,128)(2,1)}, u32[]{:S(2)}, u32[]{:S(2)}) collective-permute-start(bf16[2048,448]{0,1:T(8,128)(2,1)} %fusion.7), channel_id=1, source_target_pairs={{0,16},{16,32},{32,48},{48,64},{64,80},{80,96},{96,112},{112,128},... | collective-permute-start | bytes 5505032 | tf_op jit(solution)/shard_map/ppermute | solution.py:21
  756.3 80.5 %copy-start.1 = (bf16[2048,448]{0,1:T(8,128)(2,1)S(1)}, bf16[2048,448]{0,1:T(8,128)(2,1)}, u32[]{:S(2)}) copy-start(bf16[2048,448]{0,1:T(8,128)(2,1)} %fusion.7) | copy-start | bytes 5505028
Sparse Core Ops, SparseCore 0:
  9.8 37.5 all-gather.14
  49.9 61.5 all-gather.6
  113.9 58.1 all-gather.8
  176.5 57.8 reduce-scatter.2
  236.8 65.6 reduce-scatter.4
  304.7 40.1 all-gather.10
  346.8 150.8 all-gather.12
where the time goes:
time: 856 us; the launch traced here: 850 us
  waiting for transfers between devices  746 us (87%)
  starting transfers between devices  35.1 us (4%)
  matrix products  30.7 us (4%)
  between operations  18.7 us (2%)
  other arithmetic  18 us (2%)
    ppermute x12, waiting for transfers between devices, passed_along(): return lax.ppermute(value, axis, pairs)  300 us
    all_gather x1, waiting for transfers between devices, local(): lax.all_gather(tangent_res, 'tensor', axis=0, tiled=True)  129 us
    reduce_scatter x1, waiting for transfers between devices, local(): lax.psum_scatter(forward_term(tangent_hidden), 'tensor', scatter_dimensio...  66.4 us
    all_gather x1, waiting for transfers between devices, local(): lax.all_gather(up_weight, 'replica', axis=0, tiled=True)  60.8 us
    all_gather x1, waiting for transfers between devices, local(): down_full = lax.all_gather(down_weight, 'replica', axis=1, tiled=True)  58 us
    reduce_scatter x1, waiting for transfers between devices, local(): lax.psum_scatter(forward_term(hidden), 'tensor', scatter_dimension=0, til...  51 us
    all_gather x1, waiting for transfers between devices, local(): lax.all_gather(residual, 'tensor', axis=0, tiled=True)  40.9 us
    all_gather x1, waiting for transfers between devices, local(): gathered = lax.all_gather(tokens[0], 'tensor', axis=0, tiled=True)  38.1 us
  transfers between devices with their start and end apart: 19, of which 15 were waited for; matrix products, arithmetic and copies ran while one was open for 5% of the time, Pallas kernels for 0%

commit v1 on v0

v1 whole, which is shorter than its diff:
```python
import functools
import math

import jax
import jax.numpy as jnp
from jax import lax
from jax.experimental import pallas as pl
from jax.experimental.pallas import tpu as pltpu
from jax.sharding import PartitionSpec as P

MESH = pl.DeviceIdType.MESH
D = 2048
FF = 7168
DEN = 64
TOK = 384
COLS = 448
STEP_SIZE = 0.1
FLOOR = 0.1
DECAY = 0.75
INV_WIDTH = 1.0 / math.sqrt(D)
INV_HIDDEN = 1.0 / math.sqrt(FF)

CH = 128
NC = D // CH
PK = CH * 7 // 2
HALF = PK // 2
f32 = jnp.float32
bf16 = jnp.bfloat16


def mod(value, count):
    return lax.rem(value + 4 * count, count)


class Gather:
    def __init__(self, slot, rows, own, sems, zh, x, device):
        self.slot, self.rows, self.own = slot, rows, own
        (self.z_s, self.z_r, self.zf_s, self.zf_r, self.x_s, self.x_r, self.xf_s, self.xf_r) = sems
        self.zh, self.x, self.device = zh, x, device

    def part(self, ref, half):
        size = self.rows // 2
        return ref.at[pl.ds(half * size, size)]

    def z_copy(self, way):
        return pltpu.make_async_remote_copy(
            self.own, self.slot(self.x, self.zh), self.z_s.at[way], self.z_r.at[way],
            device_id=self.device(1 - 2 * way, 0), device_id_type=MESH)

    def z_start(self):
        for way in range(2):
            self.z_copy(way).start()

    def z_forward_copy(self, way):
        block = self.part(self.slot(self.x, mod(self.zh - (1 - 2 * way), 4)), way)
        return pltpu.make_async_remote_copy(
            block, block, self.zf_s.at[way], self.zf_r.at[way],
            device_id=self.device(1 - 2 * way, 0), device_id_type=MESH)

    def z_forward(self):
        for way in range(2):
            self.z_copy(way).wait_recv()
            self.z_forward_copy(way).start()

    def z_last(self):
        for way in range(2):
            self.z_forward_copy(way).wait_recv()

    def x_copy(self, q, way):
        block = self.slot(self.x, mod(self.zh + q, 4))
        return pltpu.make_async_remote_copy(
            self.own if q == 0 else block, block, self.x_s.at[q, way], self.x_r.at[q, way],
            device_id=self.device(0, 1 - 2 * way), device_id_type=MESH)

    def x_start(self, q):
        for way in range(2):
            self.x_copy(q, way).start()

    def x_forward_copy(self, q, way):
        block = self.part(self.slot(mod(self.x - (1 - 2 * way), 4), mod(self.zh + q, 4)), way)
        return pltpu.make_async_remote_copy(
            block, block, self.xf_s.at[q, way], self.xf_r.at[q, way],
            device_id=self.device(0, 1 - 2 * way), device_id_type=MESH)

    def x_forward(self, q):
        for way in range(2):
            self.x_copy(q, way).wait_recv()
            self.x_forward_copy(q, way).start()

    def x_last(self, q):
        for way in range(2):
            self.x_forward_copy(q, way).wait_recv()

    def drain(self):
        for way in range(2):
            self.z_copy(way).wait_send()
            self.z_forward_copy(way).wait_send()
            for q in range(4):
                self.x_copy(q, way).wait_send()
                self.x_forward_copy(q, way).wait_send()


def kernel(
    tok_ref, tgt_ref, w_hbm, p_hbm, h_hbm, up_ref, down_ref, nb_ref, num_ref,
    out_w, out_t,
    w_ref, p_ref, h_ref, tk, pair, x_all, x_turned, upb, dnb,
    gate_acc, probe_acc, up_acc, grad_acc, tang_acc,
    hid, gates, core_send, core_recv, own_part, rs_send, rs_recv, res,
    own_mix, left_mix, right_mix, far_mix, below, above, mine, staged,
    load_sem, tk_s, tk_r, tkf_s, tg_s, tg_r,
    uz_s, uz_r, uzf_s, uzf_r, ux_s, ux_r, uxf_s, uxf_r,
    dz_s, dz_r, dzf_s, dzf_r, dx_s, dx_r, dxf_s, dxf_r,
    cs_s, cs_r, rs_s, rs_r, ag_s, ag_r, ac_s, ac_r,
    mx_s, mx_r, mf_s, mf_r, mz_s, mz_r, out_sem,
):
    r = lax.axis_index("replica")
    t = lax.axis_index("tensor")
    zh, x = r // 4, lax.rem(r, 4)
    chip, core = t // 2, lax.rem(t, 2)
    sibling = (r, 2 * chip + 1 - core)

    def replica_at(dz, dx):
        return mod(zh + dz, 4) * 4 + mod(x + dx, 4)

    def device(dz, dx):
        return (replica_at(dz, dx), t)

    def peer(j):
        return (r, 2 * lax.rem(chip + j, 8) + core)

    def remote(src, dst, send, recv, where):
        return pltpu.make_async_remote_copy(
            src, dst, send, recv, device_id=where, device_id_type=MESH)

    loads = [
        pltpu.make_async_copy(src, dst, load_sem.at[i])
        for i, (src, dst) in enumerate(((w_hbm, w_ref), (p_hbm, p_ref), (h_hbm, h_ref)))
    ]
    for load in loads:
        load.start()

    barrier = pltpu.get_barrier_semaphore()
    partners = [device(1, 0), device(-1, 0), device(0, 1), device(0, -1), sibling]
    for where in partners:
        pl.semaphore_signal(barrier, inc=1, device_id=where, device_id_type=MESH)

    @pl.loop(1, 8)
    def _(j):
        pl.semaphore_signal(barrier, inc=1, device_id=peer(j), device_id_type=MESH)

    def packed_rows(ref):
        block = ref[...].astype(f32)
        return jnp.concatenate([block[:, :1024], block[:, 1024:]], axis=0).astype(bf16)

    tk[t] = packed_rows(tok_ref)
    pair[core] = packed_rows(tgt_ref)
    upb[x, zh] = up_ref[...]
    dnb[x, :, pl.ds(pl.multiple_of(zh * 128, 128), 128)] = down_ref[...]
    pl.semaphore_wait(barrier, 12)

    def tk_copy(j):
        return remote(tk.at[t], tk.at[t], tk_s.at[j], tk_r.at[j], peer(j))

    def tk_from(j):
        slot = 2 * lax.rem(chip + 8 - j, 8) + core
        return remote(tk.at[slot], tk.at[slot], tkf_s.at[j], tk_r.at[j], sibling)

    def tk_pass(j):
        slot = 2 * lax.rem(chip + 8 - j, 8) + core
        return remote(tk.at[slot], tk.at[slot], tkf_s.at[j], tk_r.at[8 + j], sibling)

    target_copy = remote(pair.at[core], pair.at[core], tg_s, tg_r, sibling)

    up_gather = Gather(lambda column, row: upb.at[column, row], 128, up_ref,
                       (uz_s, uz_r, uzf_s, uzf_r, ux_s, ux_r, uxf_s, uxf_r), zh, x, device)
    down_gather = Gather(
        lambda column, row: dnb.at[column, :, pl.ds(pl.multiple_of(row * 128, 128), 128)], COLS, down_ref,
        (dz_s, dz_r, dzf_s, dzf_r, dx_s, dx_r, dxf_s, dxf_r), zh, x, device)

    up_gather.x_start(0)
    up_gather.z_start()

    @pl.loop(1, 8)
    def _(j):
        tk_copy(j).start()

    tk_pass(0).start()
    target_copy.start()
    up_gather.z_forward()
    up_gather.x_start(1)
    up_gather.x_start(3)
    up_gather.x_forward(0)
    down_gather.z_start()
    up_gather.z_last()
    up_gather.x_start(2)

    @pl.loop(1, 8)
    def _(j):
        tk_from(j).wait_recv()
        tk_pass(j).start()

    up_gather.x_forward(1)
    up_gather.x_forward(3)
    down_gather.z_forward()
    down_gather.x_start(0)

    @pl.loop(0, 8)
    def _(j):
        tk_pass(j).wait_recv()

    @pl.loop(0, 8)
    def _(c):
        blocks = [tk[2 * c + k].astype(f32) for k in range(2)]
        rows = [jnp.concatenate([b[:24], b[24:]], axis=1) for b in blocks]
        x_all[pl.ds(pl.multiple_of(c * 48, 48), 48), :] = jnp.concatenate(rows, axis=0).astype(bf16)

    up_gather.x_forward(2)
    down_gather.x_start(1)
    down_gather.x_start(3)

    def wide_dot(acc, weight):
        @pl.loop(0, 4)
        def _(k):
            part = jnp.dot(
                x_all[:, pl.ds(pl.multiple_of(k * 512, 512), 512)],
                weight[pl.ds(pl.multiple_of(k * 512, 512), 512), :],
                preferred_element_type=f32,
            )

            @pl.when(k == 0)
            def _():
                acc[...] = part

            @pl.when(k > 0)
            def _():
                acc[...] += part

    loads[0].wait()
    wide_dot(gate_acc, w_ref)
    down_gather.z_last()
    down_gather.x_start(2)
    loads[1].wait()
    wide_dot(probe_acc, p_ref)
    down_gather.x_forward(0)

    for q in range(4):
        up_gather.x_last(q)

    @pl.loop(0, 4)
    def _(column):
        lanes = [x_all[:, pl.ds(pl.multiple_of(512 * z + 128 * column, 128), 128)] for z in range(4)]
        part = jnp.dot(
            jnp.concatenate(lanes, axis=1), upb[column].reshape(512, COLS), preferred_element_type=f32)

        @pl.when(column == 0)
        def _():
            up_acc[...] = part

        @pl.when(column > 0)
        def _():
            up_acc[...] += part

    @pl.loop(0, 8)
    def _(c):
        rows = pl.ds(pl.multiple_of(c * 48, 48), 48)
        gate_pre = gate_acc[rows, :] * INV_WIDTH
        probe_pre = probe_acc[rows, :] * INV_WIDTH
        up_pre = up_acc[rows, :] * INV_WIDTH
        logistic = jax.nn.sigmoid(gate_pre)
        slope_one = logistic * (1.0 + gate_pre * (1.0 - logistic))
        slope_two = logistic * (1.0 - logistic) * (2.0 + gate_pre * (1.0 - 2.0 * logistic))
        hid[0, rows, :] = (gate_pre * logistic * up_pre).astype(bf16)
        first = up_pre * slope_one
        hid[1, rows, :] = (first * probe_pre).astype(bf16)
        gate_acc[rows, :] = first
        probe_acc[rows, :] = up_pre * slope_two * probe_pre

    down_gather.x_forward(1)
    down_gather.x_forward(3)

    @pl.loop(0, 16)
    def _(c):
        lanes = pl.ds(pl.multiple_of(c * 128, 128), 128)
        x_turned[lanes, :] = x_all[:, lanes].astype(f32).T.astype(bf16)

    target_copy.wait_recv()
    down_gather.x_forward(2)

    columns = [mod(x + step, 4) for step in (0, 3, 1, 2)]

    def lanes_of(k):
        return pl.ds(pl.multiple_of(256 * k, 256), 256)

    def core_copy(s, p):
        return remote(core_send.at[p, s], core_recv.at[p, s], cs_s.at[p, s], cs_r.at[p, s], sibling)

    def forward(s, p):
        away = jnp.dot(hid[p], dnb[columns[s], :, lanes_of(1 - core)], preferred_element_type=f32)
        core_send[p, s] = (away * INV_HIDDEN).astype(bf16)
        core_copy(s, p).start()
        here = jnp.dot(hid[p], dnb[columns[s], :, lanes_of(core)], preferred_element_type=f32)
        own_part[p, s] = here * INV_HIDDEN

    def rs_copy(s, p, j):
        to = lax.rem(chip + j, 8)
        return remote(
            rs_send.at[p, s, pl.ds(pl.multiple_of(48 * to, 48), 48)], rs_recv.at[p, s, j],
            rs_s.at[p, s, j], rs_r.at[p, s, j], peer(j))

    def scatter(s, p):
        core_copy(s, p).wait_recv()
        total = own_part[p, s] + core_recv[p, s].astype(f32)
        own_part[p, s] = total
        rs_send[p, s] = total.astype(bf16)

        @pl.loop(1, 8)
        def _(j):
            rs_copy(s, p, j).start()

    own_rows = pl.ds(pl.multiple_of(48 * chip, 48), 48)

    def ag_copy(s, p, j):
        block = res.at[p, s, core, own_rows]
        return remote(block, block, ag_s.at[p, s, j], ag_r.at[p, s, j], peer(j))

    def reduce(s, p):
        @pl.loop(1, 8)
        def _(j):
            rs_copy(s, p, j).wait_recv()

        total = own_part[p, s, own_rows, :]
        for j in range(1, 8):
            total = total + rs_recv[p, s, j].astype(f32)
        if p == 0:
            target = []
            for k in range(2):
                block = pair[k]
                pieces = []
                for m in range(2):
                    at = pl.ds(pl.multiple_of(512 * m + 128 * columns[s], 128), 128)
                    top = pair[k, :, at].astype(f32)
                    pieces.append(jnp.where(core == 0, top[:24], top[24:]))
                target.append(jnp.concatenate(pieces, axis=1))
            total = total - jnp.concatenate(target, axis=0)
        res[p, s, core, own_rows, :] = total.astype(bf16)

        @pl.loop(1, 8)
        def _(j):
            ag_copy(s, p, j).start()

    def across_copy(s, p, k):
        return remote(res.at[p, s, k], res.at[p, s, k], ac_s.at[p, s], ac_r.at[p, s], sibling)

    def across(s, p):
        @pl.loop(1, 8)
        def _(j):
            ag_copy(s, p, j).wait_recv()

        across_copy(s, p, core).start()

    def backward(s, p, acc):
        across_copy(s, p, 1 - core).wait_recv()
        rows = jnp.concatenate([res[p, s, 0], res[p, s, 1]], axis=1)
        part = lax.dot_general(
            rows, dnb[columns[s]], (((1,), (1,)), ((), ())), preferred_element_type=f32) * INV_HIDDEN
        if s == 0:
            acc[...] = part
        else:
            acc[...] += part

    def ready(s):
        if s == 3:
            for q in range(4):
                down_gather.x_last(q)

    for step in range(8):
        for p in range(2):
            if step < 4:
                if p == 0:
                    ready(step)
                forward(step, p)
            if 0 <= step - 1 < 4:
                scatter(step - 1, p)
            if 0 <= step - 2 < 4:
                reduce(step - 2, p)
            if 0 <= step - 3 < 4:
                across(step - 3, p)
            if 0 <= step - 4 < 4:
                backward(step - 4, p, grad_acc if p == 0 else tang_acc)

    loads[2].wait()

    @pl.loop(0, 8)
    def _(c):
        rows = pl.ds(pl.multiple_of(c * 48, 48), 48)
        grad = grad_acc[rows, :]
        gates[0, rows, :] = (grad * gate_acc[rows, :]).astype(bf16)
        gates[1, rows, :] = (tang_acc[rows, :] * gate_acc[rows, :] + grad * probe_acc[rows, :]).astype(bf16)

    def share(dest, source):
        total = jnp.int32(0)
        for k in range(6):
            total = total + jnp.where(nb_ref[dest, k] == source, num_ref[dest, k], 0)
        return total.astype(f32) * (1.0 / DEN)

    def self_share():
        total = jnp.int32(0)
        for k in range(6):
            total = total + num_ref[r, k]
        return (DEN - total).astype(f32) * (1.0 / DEN)

    sources = [replica_at(0, dx) for dx in (0, -1, 1, 2)]
    here_c = [self_share()] + [share(r, source) for source in sources[1:]]
    up_c = [share(replica_at(1, 0), source) for source in sources]
    down_c = [share(replica_at(-1, 0), source) for source in sources]

    def product(path, rows):
        return jnp.dot(x_turned[rows, :], gates[path], preferred_element_type=f32) * INV_WIDTH

    def put(g, value):
        for b in range(3):
            own_mix[g, pl.ds(b * CH, CH), :] = value[:, 128 * b : 128 * (b + 1)].astype(bf16)
        tail = jnp.concatenate([value[: CH // 2, 384:], value[CH // 2 :, 384:]], axis=1)
        own_mix[g, pl.ds(3 * CH, CH // 2), :] = tail.astype(bf16)

    def produce_step(i):
        rows = pl.ds(pl.multiple_of(i * CH, CH), CH)
        ratio = product(0, rows) / jnp.maximum(h_ref[rows, :].astype(f32), FLOOR)
        put(i, w_ref[rows, :].astype(f32) - STEP_SIZE * jnp.clip(ratio, -1.0, 1.0))

    def produce_track(i):
        rows = pl.ds(pl.multiple_of(i * CH, CH), CH)
        curvature = product(1, rows)
        put(NC + i, DECAY * h_ref[rows, :].astype(f32) + (1.0 - DECAY) * p_ref[rows, :].astype(f32) * curvature)

    def mx_copy(g, way):
        return remote(
            own_mix.at[g], (left_mix if way == 0 else right_mix).at[g],
            mx_s.at[g, way], mx_r.at[g, way], device(0, 1 - 2 * way))

    def mf_copy(g, way):
        part = pl.ds(way * HALF, HALF)
        return remote(
            (left_mix if way == 0 else right_mix).at[g, part], far_mix.at[g, part],
            mf_s.at[g, way], mf_r.at[g, way], device(0, 1 - 2 * way))

    def mz_copy(g, way):
        return remote(
            (left_mix if way == 0 else right_mix).at[g], (below if way == 0 else above).at[g],
            mz_s.at[g, way], mz_r.at[g, way], device(1 - 2 * way, 0))

    def x_send(g):
        for way in range(2):
            mx_copy(g, way).start()

    def x_pass(g):
        for way in range(2):
            mx_copy(g, way).wait_recv()
            mf_copy(g, way).start()

    def z_send(g):
        for way in range(2):
            mf_copy(g, way).wait_recv()
            mf_copy(g, way).wait_send()
        slot = lax.rem(g, 4)

        @pl.loop(0, 4)
        def _(piece):
            rows = pl.ds(pl.multiple_of(piece * (PK // 4), 16), PK // 4)
            parts = [ref[g, rows, :].astype(f32) for ref in (own_mix, left_mix, right_mix, far_mix)]

            def weighted(shares):
                total = shares[0] * parts[0]
                for c, part in zip(shares[1:], parts[1:]):
                    total = total + c * part
                return total

            mine[slot, rows, :] = weighted(here_c)
            left_mix[g, rows, :] = weighted(up_c).astype(bf16)
            right_mix[g, rows, :] = weighted(down_c).astype(bf16)

        for way in range(2):
            mz_copy(g, way).start()

    def out_copy(out, i, slot):
        return pltpu.make_async_copy(
            staged.at[slot], out.at[pl.ds(pl.multiple_of(i * CH, CH), CH)], out_sem.at[slot])

    def finish(out, i, g):
        for way in range(2):
            mz_copy(g, way).wait_recv()
        total = mine[lax.rem(g, 4)] + below[g].astype(f32) + above[g].astype(f32)
        slot = lax.rem(g, 2)

        @pl.when(g >= 2)
        def _():
            out_copy(out, i, slot).wait()

        for b in range(3):
            staged[slot, :, pl.ds(128 * b, 128)] = total[b * CH : (b + 1) * CH].astype(bf16)
        tail = total[3 * CH :]
        last = jnp.concatenate([tail[:, :64], tail[:, 64:]], axis=0)
        staged[slot, :, pl.ds(384, 64)] = last.astype(bf16)
        out_copy(out, i, slot).start()

    produce_step(0)
    x_send(0)
    produce_step(1)
    x_send(1)
    x_pass(0)

    @pl.loop(0, 2 * NC + 2)
    def _(g):
        @pl.when(g + 2 < NC)
        def _():
            produce_step(g + 2)

        @pl.when((g + 2 >= NC) & (g + 2 < 2 * NC))
        def _():
            produce_track(g + 2 - NC)

        @pl.when(g + 2 < 2 * NC)
        def _():
            x_send(g + 2)

        @pl.when(g + 1 < 2 * NC)
        def _():
            x_pass(g + 1)

        @pl.when(g < 2 * NC)
        def _():
            z_send(g)

        @pl.when((g >= 2) & (g < NC + 2))
        def _():
            finish(out_w, g - 2, g - 2)

        @pl.when(g >= NC + 2)
        def _():
            finish(out_t, g - 2 - NC, g - 2)

    for slot in range(2):
        out_copy(out_t, 0, slot).wait()
    up_gather.drain()
    down_gather.drain()
    target_copy.wait_send()

    @pl.loop(0, 8)
    def _(j):
        tk_pass(j).wait_send()

    @pl.loop(1, 8)
    def _(j):
        tk_copy(j).wait_send()
        for s in range(4):
            for p in range(2):
                rs_copy(s, p, j).wait_send()
                ag_copy(s, p, j).wait_send()

    for s in range(4):
        for p in range(2):
            core_copy(s, p).wait_send()
            across_copy(s, p, core).wait_send()

    @pl.loop(0, 2 * NC)
    def _(g):
        for way in range(2):
            mx_copy(g, way).wait_send()
            mz_copy(g, way).wait_send()


def local(
    tokens, targets, gate_weight, probes, tracker, up_weight, down_weight, neighbours, numerators
):
    vmem = pl.BlockSpec(memory_space=pltpu.VMEM)
    hbm = pl.BlockSpec(memory_space=pl.ANY)
    smem = pl.BlockSpec(memory_space=pltpu.SMEM)
    dma = pltpu.SemaphoreType.DMA
    weight = jax.ShapeDtypeStruct((D, COLS), bf16)
    wide = pltpu.VMEM((TOK, COLS), f32)
    mixed = pltpu.VMEM((2 * NC, PK, 128), bf16)
    gather_sems = [dma((2,))] * 4 + [dma((4, 2))] * 4
    mixed_weights, mixed_tracker = pl.pallas_call(
        kernel,
        out_shape=(weight, weight),
        in_specs=[vmem, vmem, hbm, hbm, hbm, vmem, vmem, smem, smem],
        out_specs=(hbm, hbm),
        scratch_shapes=[
            pltpu.VMEM((D, COLS), bf16),
            pltpu.VMEM((D, COLS), bf16),
            pltpu.VMEM((D, COLS), bf16),
            pltpu.VMEM((16, 48, 1024), bf16),
            pltpu.VMEM((2, 48, 1024), bf16),
            pltpu.VMEM((TOK, D), bf16),
            pltpu.VMEM((D, TOK), bf16),
            pltpu.VMEM((4, 4, 128, COLS), bf16),
            pltpu.VMEM((4, COLS, 512), bf16),
            wide, wide, wide, wide, wide,
            pltpu.VMEM((2, TOK, COLS), bf16),
            pltpu.VMEM((2, TOK, COLS), bf16),
            pltpu.VMEM((2, 4, TOK, 256), bf16),
            pltpu.VMEM((2, 4, TOK, 256), bf16),
            pltpu.VMEM((2, 4, TOK, 256), f32),
            pltpu.VMEM((2, 4, TOK, 256), bf16),
            pltpu.VMEM((2, 4, 8, 48, 256), bf16),
            pltpu.VMEM((2, 4, 2, TOK, 256), bf16),
            mixed, mixed, mixed, mixed, mixed, mixed,
            pltpu.VMEM((4, PK, 128), f32),
            pltpu.VMEM((2, CH, COLS), bf16),
            dma((3,)), dma((8,)), dma((16,)), dma((8,)), dma, dma,
            *gather_sems, *gather_sems,
            dma((2, 4)), dma((2, 4)), dma((2, 4, 8)), dma((2, 4, 8)),
            dma((2, 4, 8)), dma((2, 4, 8)), dma((2, 4)), dma((2, 4)),
            dma((2 * NC, 2)), dma((2 * NC, 2)), dma((2 * NC, 2)), dma((2 * NC, 2)),
            dma((2 * NC, 2)), dma((2 * NC, 2)), dma((2,)),
        ],
        compiler_params=pltpu.CompilerParams(
            collective_id=0, has_side_effects=True, vmem_limit_bytes=63 << 20
        ),
        name="step_and_mix",
    )(
        tokens[0], targets[0], gate_weight[0], probes[0], tracker[0], up_weight, down_weight,
        neighbours, numerators,
    )
    return (mixed_weights[None], mixed_tracker[None])


def solution(mesh):
    return jax.shard_map(
        local,
        mesh=mesh,
        in_specs=(
            P("replica", "tensor", None),
            P("replica", "tensor", None),
            P("replica", None, "tensor"),
            P("replica", None, "tensor"),
            P("replica", None, "tensor"),
            P("replica", "tensor"),
            P("tensor", "replica"),
            P(),
            P(),
        ),
        out_specs=(P("replica", None, "tensor"), P("replica", None, "tensor")),
        check_vma=False,
    )
```

time: 856 us -> 295 us (0.34)
  waiting for transfers between devices: 746 us -> 0 us
  Pallas kernels: 0 us -> 271 us
  starting transfers between devices: 35.1 us -> 0 us
  matrix products: 30.7 us -> 0 us
  local copies, waits for them, and re-layouts: 0.88 us -> 20.9 us
  between operations: 18.7 us -> 0.65 us
  other arithmetic: 18 us -> 0 us
    all_gather x5 -> x0, waiting for transfers between devices: 326 us -> none  [the longest x1 129 us: local(): lax.all_gather(tangent_res, 'tensor', axis=0, tiled=True)]
    ppermute x12 -> x0, waiting for transfers between devices: 300 us -> none  [passed_along(): return lax.ppermute(value, axis, pairs)]
    pallas_call x0 -> x1, Pallas kernels: none -> 271 us  [local(): pl.pallas_call(kernel, out_shape=(weight, weight), in_specs=[vmem, vmem,...]
    reduce_scatter x2 -> x0, waiting for transfers between devices: 117 us -> none  [the longest x1 66.4 us: local(): lax.psum_scatter(forward_term(tangent_hidden), 'tensor', scatter_dimensio...]
    ppermute x12 -> x0, starting transfers between devices: 34.9 us -> none  [passed_along(): return lax.ppermute(value, axis, pairs)]
    dot_general x8 -> x0, matrix products: 30.7 us -> none  [the longest x1 7.23 us: local(): lax.dot_general(gathered, tangent_gate, (((0,), (0,)), ((), ())), preferr...]
    unnamed x22 -> x12, local copies, waits for them, and re-layouts: 0.88 us -> 20.9 us
    broadcast_in_dim x2 -> x0, other arithmetic: 13.3 us -> none  [local(): return (mixed_weights[None], mixed_tracker[None])]
  transfers between devices with their start and end apart: 19 -> 0, of which waited for: 15 -> 0; matrix products, arithmetic and copies ran while one was open for 5% -> 0% of each run, Pallas kernels for 0% -> 0%
where the time goes in v1:
time: 295 us; the launch traced here: 292 us
  Pallas kernels  271 us (92%)
  local copies, waits for them, and re-layouts  20.9 us (7%)
    pallas_call x1, Pallas kernels, local(): pl.pallas_call(kernel, out_shape=(weight, weight), in_specs=[vmem, vmem,...  271 us
    unnamed x12, local copies, waits for them, and re-layouts  20.9 us

profile of v1, /device:TPU:16, one launch (start us, length us, event | category | flops | bytes accessed | tf_op | source)
XLA Modules:
  0.0 292.2 jit_solution(2527265473307604752)
XLA Ops:
  0.6 1.4 copy.15.nb_ref
  2.0 0.0 copy-start.1
  2.0 1.5 copy.16.num_ref
  3.5 1.7 copy.14.up_ref
  5.1 3.8 %copy.11 = bf16[1,2048,448]{2,1,0:T(8,128)(2,1)} copy(bf16[1,2048,448]{1,2,0:T(8,128)(2,1)} %param.11) | data formatting | bytes 3670016 | tf_op args[2]
  9.0 0.0 copy-done.1
  9.0 2.4 copy.12
  11.4 3.8 %copy.13 = bf16[1,2048,448]{2,1,0:T(8,128)(2,1)} copy(bf16[1,2048,448]{1,2,0:T(8,128)(2,1)} %param.13) | data formatting | bytes 3670016 | tf_op args[4]
  15.2 270.7 %step_and_mix.1 = (bf16[2048,448]{1,0:T(8,128)(2,1)}, bf16[2048,448]{1,0:T(8,128)(2,1)}) custom-call(bf16[24,2048]{1,0:T(8,128)(2,1)} %bitcast.12, bf16[24,2048]{1,0:T(8,128)(2,1)} %bitcast.13, bf16[2048,448]{1,0:T(8,128)(2,1)} %bitcast.7, bf16[2048,448]{1,0:T(8,128)(2,1)} %bitcast.8, bf16[2048,448]{1,0:T(8,128)(2,1)} %bitcast.9, ...), custom_call_target="tpu_custom_call" | custom-call | tf_op jit(solution)/shard_map/step_and_mix/pallas_call | solution.py:583
  285.9 0.0 copy-start
  285.9 4.0 %copy.17 = bf16[1,2048,448]{1,2,0:T(8,128)(2,1)} copy(bf16[1,2048,448]{2,1,0:T(8,128)(2,1)} %bitcast.11) | data formatting | bytes 3670016
  289.9 0.0 copy-done
  289.9 2.3 copy.18
Async XLA Ops:
  2.0 7.0 %copy-start.1 = (bf16[1,2048,448]{1,2,0:T(8,128)(2,1)S(1)}, bf16[1,2048,448]{1,2,0:T(8,128)(2,1)}, u32[]{:S(2)}) copy-start(bf16[1,2048,448]{1,2,0:T(8,128)(2,1)} %param.12) | copy-start | bytes 5505028
  285.9 4.0 %copy-start = (bf16[2048,448]{1,0:T(8,128)(2,1)S(1)}, bf16[2048,448]{1,0:T(8,128)(2,1)}, u32[]{:S(2)}) copy-start(bf16[2048,448]{1,0:T(8,128)(2,1)} %get-tuple-element.5) | copy-start | bytes 5505028

commit v2 on v1

--- a/solution.py
+++ b/solution.py
@@ -22,8 +22,7 @@
 
 CH = 128
 NC = D // CH
-PK = CH * 7 // 2
-HALF = PK // 2
+HALF = COLS // 2
 f32 = jnp.float32
 bf16 = jnp.bfloat16
 
@@ -103,20 +102,21 @@
 def kernel(
     tok_ref, tgt_ref, w_hbm, p_hbm, h_hbm, up_ref, down_ref, nb_ref, num_ref,
     out_w, out_t,
-    w_ref, p_ref, h_ref, tk, pair, x_all, x_turned, upb, dnb,
-    gate_acc, probe_acc, up_acc, grad_acc, tang_acc,
-    hid, gates, core_send, core_recv, own_part, rs_send, rs_recv, res,
+    w_ref, p_ref, h_ref, tk, pair, x_all, upb, dnb,
+    gate_acc, probe_acc, up_acc, first_turned, second_turned, grad_acc, tang_acc,
+    hid, gates, core_send, core_recv, own_part, rs_send, rs_recv, pair_send, pair_recv, res,
     own_mix, left_mix, right_mix, far_mix, below, above, mine, staged,
     load_sem, tk_s, tk_r, tkf_s, tg_s, tg_r,
     uz_s, uz_r, uzf_s, uzf_r, ux_s, ux_r, uxf_s, uxf_r,
     dz_s, dz_r, dzf_s, dzf_r, dx_s, dx_r, dxf_s, dxf_r,
-    cs_s, cs_r, rs_s, rs_r, ag_s, ag_r, ac_s, ac_r,
+    cs_s, cs_r, rs_s, rs_r, pair_s, pair_r, ag_s, ag_r, ac_s, ac_r,
     mx_s, mx_r, mf_s, mf_r, mz_s, mz_r, out_sem,
 ):
     r = lax.axis_index("replica")
     t = lax.axis_index("tensor")
     zh, x = r // 4, lax.rem(r, 4)
     chip, core = t // 2, lax.rem(t, 2)
+    half, y = chip // 4, lax.rem(chip, 4)
     sibling = (r, 2 * chip + 1 - core)
 
     def replica_at(dz, dx):
@@ -127,6 +127,12 @@
 
     def peer(j):
         return (r, 2 * lax.rem(chip + j, 8) + core)
+
+    def chip_at(a, b):
+        return 4 * lax.rem(half + a, 2) + mod(y + b, 4)
+
+    def same_core(a, b):
+        return (r, 2 * chip_at(a, b) + core)
 
     def remote(src, dst, send, recv, where):
         return pltpu.make_async_remote_copy(
@@ -155,58 +161,67 @@
     tk[t] = packed_rows(tok_ref)
     pair[core] = packed_rows(tgt_ref)
     upb[x, zh] = up_ref[...]
-    dnb[x, :, pl.ds(pl.multiple_of(zh * 128, 128), 128)] = down_ref[...]
+    dnb[x, zh] = down_ref[...]
     pl.semaphore_wait(barrier, 12)
 
-    def tk_copy(j):
-        return remote(tk.at[t], tk.at[t], tk_s.at[j], tk_r.at[j], peer(j))
-
-    def tk_from(j):
-        slot = 2 * lax.rem(chip + 8 - j, 8) + core
-        return remote(tk.at[slot], tk.at[slot], tkf_s.at[j], tk_r.at[j], sibling)
-
-    def tk_pass(j):
-        slot = 2 * lax.rem(chip + 8 - j, 8) + core
-        return remote(tk.at[slot], tk.at[slot], tkf_s.at[j], tk_r.at[8 + j], sibling)
+    def tk_slot(a, b):
+        return tk.at[2 * chip_at(a, b) + core]
+
+    def tk_copy(a, b):
+        block = tk_slot(a, 0) if b else tk_slot(0, 0)
+        where = same_core(0, b) if b else same_core(1, 0)
+        return remote(block, block, tk_s.at[4 * a + b], tk_r.at[4 * a + b], where)
+
+    def tk_pass(a, b):
+        block = tk_slot(a, -b)
+        return remote(block, block, tkf_s.at[4 * a + b], tk_r.at[8 + 4 * a + b], sibling)
 
     target_copy = remote(pair.at[core], pair.at[core], tg_s, tg_r, sibling)
 
-    up_gather = Gather(lambda column, row: upb.at[column, row], 128, up_ref,
-                       (uz_s, uz_r, uzf_s, uzf_r, ux_s, ux_r, uxf_s, uxf_r), zh, x, device)
+    def slots(ref):
+        return lambda column, row: ref.at[column, row]
+
+    up_gather = Gather(
+        slots(upb), COLS, up_ref,
+        (uz_s, uz_r, uzf_s, uzf_r, ux_s, ux_r, uxf_s, uxf_r), zh, x, device)
     down_gather = Gather(
-        lambda column, row: dnb.at[column, :, pl.ds(pl.multiple_of(row * 128, 128), 128)], COLS, down_ref,
+        slots(dnb), COLS, down_ref,
         (dz_s, dz_r, dzf_s, dzf_r, dx_s, dx_r, dxf_s, dxf_r), zh, x, device)
 
+    tk_copy(1, 0).start()
+    for b in range(1, 4):
+        tk_copy(0, b).start()
+    up_gather.z_start()
     up_gather.x_start(0)
-    up_gather.z_start()
-
-    @pl.loop(1, 8)
-    def _(j):
-        tk_copy(j).start()
-
-    tk_pass(0).start()
+    tk_pass(0, 0).start()
     target_copy.start()
+
+    tk_copy(1, 0).wait_recv()
+    for b in range(1, 4):
+        tk_copy(1, b).start()
+    tk_pass(1, 0).start()
     up_gather.z_forward()
     up_gather.x_start(1)
     up_gather.x_start(3)
+    down_gather.z_start()
     up_gather.x_forward(0)
-    down_gather.z_start()
+    for b in range(1, 4):
+        tk_copy(0, b).wait_recv()
+        tk_pass(0, b).start()
     up_gather.z_last()
     up_gather.x_start(2)
-
-    @pl.loop(1, 8)
-    def _(j):
-        tk_from(j).wait_recv()
-        tk_pass(j).start()
-
+    down_gather.x_start(0)
     up_gather.x_forward(1)
     up_gather.x_forward(3)
+    for b in range(1, 4):
+        tk_copy(1, b).wait_recv()
+        tk_pass(1, b).start()
     down_gather.z_forward()
-    down_gather.x_start(0)
-
-    @pl.loop(0, 8)
-    def _(j):
-        tk_pass(j).wait_recv()
+    down_gather.x_start(1)
+    down_gather.x_start(3)
+    for a in range(2):
+        for b in range(4):
+            tk_pass(a, b).wait_recv()
 
     @pl.loop(0, 8)
     def _(c):
@@ -215,33 +230,23 @@
         x_all[pl.ds(pl.multiple_of(c * 48, 48), 48), :] = jnp.concatenate(rows, axis=0).astype(bf16)
 
     up_gather.x_forward(2)
-    down_gather.x_start(1)
-    down_gather.x_start(3)
+
+    def joined(ref, column, first, count):
+        return jnp.concatenate([ref[column, first + i] for i in range(count)], axis=1)
+
+    def rows_dot(left, right):
+        return lax.dot_general(left, right, (((1,), (1,)), ((), ())), preferred_element_type=f32)
 
     def wide_dot(acc, weight):
-        @pl.loop(0, 4)
-        def _(k):
-            part = jnp.dot(
-                x_all[:, pl.ds(pl.multiple_of(k * 512, 512), 512)],
-                weight[pl.ds(pl.multiple_of(k * 512, 512), 512), :],
-                preferred_element_type=f32,
-            )
-
-            @pl.when(k == 0)
-            def _():
-                acc[...] = part
-
-            @pl.when(k > 0)
-            def _():
-                acc[...] += part
+        acc[...] = rows_dot(x_all[...], weight[...])
 
     loads[0].wait()
     wide_dot(gate_acc, w_ref)
     down_gather.z_last()
     down_gather.x_start(2)
+    down_gather.x_forward(0)
     loads[1].wait()
     wide_dot(probe_acc, p_ref)
-    down_gather.x_forward(0)
 
     for q in range(4):
         up_gather.x_last(q)
@@ -249,8 +254,7 @@
     @pl.loop(0, 4)
     def _(column):
         lanes = [x_all[:, pl.ds(pl.multiple_of(512 * z + 128 * column, 128), 128)] for z in range(4)]
-        part = jnp.dot(
-            jnp.concatenate(lanes, axis=1), upb[column].reshape(512, COLS), preferred_element_type=f32)
+        part = rows_dot(jnp.concatenate(lanes, axis=1), joined(upb, column, 0, 4))
 
         @pl.when(column == 0)
         def _():
@@ -278,40 +282,38 @@
     down_gather.x_forward(1)
     down_gather.x_forward(3)
 
-    @pl.loop(0, 16)
-    def _(c):
-        lanes = pl.ds(pl.multiple_of(c * 128, 128), 128)
-        x_turned[lanes, :] = x_all[:, lanes].astype(f32).T.astype(bf16)
-
     target_copy.wait_recv()
     down_gather.x_forward(2)
 
     columns = [mod(x + step, 4) for step in (0, 3, 1, 2)]
 
-    def lanes_of(k):
-        return pl.ds(pl.multiple_of(256 * k, 256), 256)
+    def column(s, p):
+        return columns[s] if p == 0 else lax.rem(x + s, 4)
 
     def core_copy(s, p):
         return remote(core_send.at[p, s], core_recv.at[p, s], cs_s.at[p, s], cs_r.at[p, s], sibling)
 
     def forward(s, p):
-        away = jnp.dot(hid[p], dnb[columns[s], :, lanes_of(1 - core)], preferred_element_type=f32)
+        away = jnp.dot(hid[p], joined(dnb, column(s, p), 2 * (1 - core), 2), preferred_element_type=f32)
         core_send[p, s] = (away * INV_HIDDEN).astype(bf16)
         core_copy(s, p).start()
-        here = jnp.dot(hid[p], dnb[columns[s], :, lanes_of(core)], preferred_element_type=f32)
+        here = jnp.dot(hid[p], joined(dnb, column(s, p), 2 * core, 2), preferred_element_type=f32)
         own_part[p, s] = here * INV_HIDDEN
 
     def rs_copy(s, p, j):
         to = lax.rem(chip + j, 8)
         return remote(
-            rs_send.at[p, s, pl.ds(pl.multiple_of(48 * to, 48), 48)], rs_recv.at[p, s, j],
+            rs_send.at[p, s, to // 4, pl.ds(pl.multiple_of(48 * lax.rem(to, 4), 48), 48)], rs_recv.at[p, s, j],
             rs_s.at[p, s, j], rs_r.at[p, s, j], peer(j))
 
-    def scatter(s, p):
+    def core_sum(s, p):
         core_copy(s, p).wait_recv()
         total = own_part[p, s] + core_recv[p, s].astype(f32)
         own_part[p, s] = total
-        rs_send[p, s] = total.astype(bf16)
+        rs_send[p, s] = total.astype(bf16).reshape(2, TOK // 2, 256)
+
+    def scatter(s, p):
+        core_sum(s, p)
 
         @pl.loop(1, 8)
         def _(j):
@@ -331,17 +333,15 @@
         total = own_part[p, s, own_rows, :]
         for j in range(1, 8):
             total = total + rs_recv[p, s, j].astype(f32)
-        if p == 0:
-            target = []
-            for k in range(2):
-                block = pair[k]
-                pieces = []
-                for m in range(2):
-                    at = pl.ds(pl.multiple_of(512 * m + 128 * columns[s], 128), 128)
-                    top = pair[k, :, at].astype(f32)
-                    pieces.append(jnp.where(core == 0, top[:24], top[24:]))
-                target.append(jnp.concatenate(pieces, axis=1))
-            total = total - jnp.concatenate(target, axis=0)
+        target = []
+        for k in range(2):
+            pieces = []
+            for m in range(2):
+                at = pl.ds(pl.multiple_of(512 * m + 128 * columns[s], 128), 128)
+                top = pair[k, :, at].astype(f32)
+                pieces.append(jnp.where(core == 0, top[:24], top[24:]))
+            target.append(jnp.concatenate(pieces, axis=1))
+        total = total - jnp.concatenate(target, axis=0)
         res[p, s, core, own_rows, :] = total.astype(bf16)
 
         @pl.loop(1, 8)
@@ -361,12 +361,72 @@
     def backward(s, p, acc):
         across_copy(s, p, 1 - core).wait_recv()
         rows = jnp.concatenate([res[p, s, 0], res[p, s, 1]], axis=1)
-        part = lax.dot_general(
-            rows, dnb[columns[s]], (((1,), (1,)), ((), ())), preferred_element_type=f32) * INV_HIDDEN
-        if s == 0:
+        part = rows_dot(joined(dnb, column(s, p), 0, 4), rows) * INV_HIDDEN
+        if p == 0 and s == 0:
             acc[...] = part
         else:
             acc[...] += part
+
+    def y_copy(s, b):
+        rows = pl.ds(pl.multiple_of(48 * mod(y + b, 4), 48), 48)
+        return remote(
+            rs_send.at[1, s, :, rows], rs_recv.at[1, s, pl.ds(2 * b, 2)],
+            rs_s.at[1, s, b], rs_r.at[1, s, b], same_core(0, b))
+
+    def pair_copy(s):
+        return remote(pair_send.at[s], pair_recv.at[s], pair_s.at[s], pair_r.at[s], same_core(1, 0))
+
+    def y_scatter(s):
+        core_sum(s, 1)
+        for b in range(1, 4):
+            y_copy(s, b).start()
+
+    def y_reduce(s):
+        for b in range(1, 4):
+            y_copy(s, b).wait_recv()
+
+        def total(at):
+            value = own_part[1, s, pl.ds(pl.multiple_of(48 * (4 * at + y), 48), 48), :]
+            for b in range(1, 4):
+                value = value + rs_recv[1, s, 2 * b + at].astype(f32)
+            return value
+
+        pair_send[s] = total(1 - half).astype(bf16)
+        pair_copy(s).start()
+        own_part[1, s, own_rows, :] = total(half)
+
+    def t_copy(s, a, b):
+        at = chip_at(a, 0) if b else chip
+        block = res.at[1, s, core, pl.ds(pl.multiple_of(48 * at, 48), 48)]
+        where = same_core(0, b) if b else same_core(1, 0)
+        return remote(block, block, ag_s.at[1, s, 4 * a + b], ag_r.at[1, s, 4 * a + b], where)
+
+    def pair_reduce(s):
+        pair_copy(s).wait_recv()
+        total = own_part[1, s, own_rows, :] + pair_recv[s].astype(f32)
+        res[1, s, core, own_rows, :] = total.astype(bf16)
+        t_copy(s, 1, 0).start()
+        for b in range(1, 4):
+            t_copy(s, 0, b).start()
+
+    def pair_pass(s):
+        t_copy(s, 1, 0).wait_recv()
+        for b in range(1, 4):
+            t_copy(s, 1, b).start()
+
+    def t_across(s):
+        for a in range(2):
+            for b in range(1, 4):
+                t_copy(s, a, b).wait_recv()
+        across_copy(s, 1, core).start()
+
+    def turn(p):
+        source, turned = ((gate_acc, first_turned), (probe_acc, second_turned))[p]
+
+        @pl.loop(0, 3)
+        def _(c):
+            tokens_at = pl.ds(pl.multiple_of(c * 128, 128), 128)
+            turned[:, tokens_at] = source[tokens_at, :].T
 
     def ready(s):
         if s == 3:
@@ -374,39 +434,56 @@
                 down_gather.x_last(q)
 
     for step in range(8):
-        for p in range(2):
-            if step < 4:
-                if p == 0:
-                    ready(step)
-                forward(step, p)
-            if 0 <= step - 1 < 4:
-                scatter(step - 1, p)
-            if 0 <= step - 2 < 4:
-                reduce(step - 2, p)
-            if 0 <= step - 3 < 4:
-                across(step - 3, p)
-            if 0 <= step - 4 < 4:
-                backward(step - 4, p, grad_acc if p == 0 else tang_acc)
+        if step < 4:
+            ready(step)
+            forward(step, 0)
+        if 0 <= step - 1 < 4:
+            scatter(step - 1, 0)
+        if step in (4, 5):
+            turn(step - 4)
+        if 0 <= step - 2 < 4:
+            reduce(step - 2, 0)
+        if 0 <= step - 3 < 4:
+            across(step - 3, 0)
+        if 0 <= step - 4 < 4:
+            backward(step - 4, 0, grad_acc)
 
     loads[2].wait()
-
-    @pl.loop(0, 8)
+    tang_acc[...] = jnp.zeros_like(tang_acc)
+
+    @pl.loop(0, 7)
     def _(c):
-        rows = pl.ds(pl.multiple_of(c * 48, 48), 48)
-        grad = grad_acc[rows, :]
-        gates[0, rows, :] = (grad * gate_acc[rows, :]).astype(bf16)
-        gates[1, rows, :] = (tang_acc[rows, :] * gate_acc[rows, :] + grad * probe_acc[rows, :]).astype(bf16)
+        rows = pl.ds(pl.multiple_of(c * 64, 64), 64)
+        gates[0, rows, :] = (grad_acc[rows, :] * first_turned[rows, :]).astype(bf16)
+
+    def tangent_gates():
+        @pl.loop(0, 7)
+        def _(c):
+            rows = pl.ds(pl.multiple_of(c * 64, 64), 64)
+            gates[1, rows, :] = (
+                tang_acc[rows, :] * first_turned[rows, :] + grad_acc[rows, :] * second_turned[rows, :]
+            ).astype(bf16)
+
+    tangent_steps = (
+        lambda s: forward(s, 1),
+        y_scatter,
+        y_reduce,
+        pair_reduce,
+        pair_pass,
+        t_across,
+        lambda s: backward(s, 1, tang_acc),
+    )
 
     def share(dest, source):
         total = jnp.int32(0)
         for k in range(6):
-            total = total + jnp.where(nb_ref[dest, k] == source, num_ref[dest, k], 0)
+            total = total + jnp.where(nb_ref[k, dest] == source, num_ref[k, dest], 0)
         return total.astype(f32) * (1.0 / DEN)
 
     def self_share():
         total = jnp.int32(0)
         for k in range(6):
-            total = total + num_ref[r, k]
+            total = total + num_ref[k, r]
         return (DEN - total).astype(f32) * (1.0 / DEN)
 
     sources = [replica_at(0, dx) for dx in (0, -1, 1, 2)]
@@ -414,24 +491,17 @@
     up_c = [share(replica_at(1, 0), source) for source in sources]
     down_c = [share(replica_at(-1, 0), source) for source in sources]
 
-    def product(path, rows):
-        return jnp.dot(x_turned[rows, :], gates[path], preferred_element_type=f32) * INV_WIDTH
-
-    def put(g, value):
-        for b in range(3):
-            own_mix[g, pl.ds(b * CH, CH), :] = value[:, 128 * b : 128 * (b + 1)].astype(bf16)
-        tail = jnp.concatenate([value[: CH // 2, 384:], value[CH // 2 :, 384:]], axis=1)
-        own_mix[g, pl.ds(3 * CH, CH // 2), :] = tail.astype(bf16)
-
-    def produce_step(i):
-        rows = pl.ds(pl.multiple_of(i * CH, CH), CH)
-        ratio = product(0, rows) / jnp.maximum(h_ref[rows, :].astype(f32), FLOOR)
-        put(i, w_ref[rows, :].astype(f32) - STEP_SIZE * jnp.clip(ratio, -1.0, 1.0))
-
-    def produce_track(i):
-        rows = pl.ds(pl.multiple_of(i * CH, CH), CH)
-        curvature = product(1, rows)
-        put(NC + i, DECAY * h_ref[rows, :].astype(f32) + (1.0 - DECAY) * p_ref[rows, :].astype(f32) * curvature)
+    def produce(path, pair_at):
+        lanes = pl.ds(pl.multiple_of(pair_at * 256, 256), 256)
+        change = jnp.dot(gates[path], x_all[:, lanes], preferred_element_type=f32) * INV_WIDTH
+        old = h_ref[:, lanes].astype(f32)
+        if path == 0:
+            ratio = change / jnp.maximum(old, FLOOR)
+            new = w_ref[:, lanes].astype(f32) - STEP_SIZE * jnp.clip(ratio, -1.0, 1.0)
+        else:
+            new = DECAY * old + (1.0 - DECAY) * p_ref[:, lanes].astype(f32) * change
+        for m in range(2):
+            own_mix[path * NC + 2 * pair_at + m] = new[:, 128 * m : 128 * (m + 1)].astype(bf16)
 
     def mx_copy(g, way):
         return remote(
@@ -466,7 +536,7 @@
 
         @pl.loop(0, 4)
         def _(piece):
-            rows = pl.ds(pl.multiple_of(piece * (PK // 4), 16), PK // 4)
+            rows = pl.ds(pl.multiple_of(piece * (COLS // 4), 16), COLS // 4)
             parts = [ref[g, rows, :].astype(f32) for ref in (own_mix, left_mix, right_mix, far_mix)]
 
             def weighted(shares):
@@ -484,7 +554,7 @@
 
     def out_copy(out, i, slot):
         return pltpu.make_async_copy(
-            staged.at[slot], out.at[pl.ds(pl.multiple_of(i * CH, CH), CH)], out_sem.at[slot])
+            staged.at[slot], out.at[:, pl.ds(pl.multiple_of(i * CH, CH), CH)], out_sem.at[slot])
 
     def finish(out, i, g):
         for way in range(2):
@@ -496,28 +566,26 @@
         def _():
             out_copy(out, i, slot).wait()
 
-        for b in range(3):
-            staged[slot, :, pl.ds(128 * b, 128)] = total[b * CH : (b + 1) * CH].astype(bf16)
-        tail = total[3 * CH :]
-        last = jnp.concatenate([tail[:, :64], tail[:, 64:]], axis=0)
-        staged[slot, :, pl.ds(384, 64)] = last.astype(bf16)
+        staged[slot] = total.astype(bf16)
         out_copy(out, i, slot).start()
 
-    produce_step(0)
+    produce(0, 0)
     x_send(0)
-    produce_step(1)
     x_send(1)
+    produce(0, 1)
     x_pass(0)
 
     @pl.loop(0, 2 * NC + 2)
     def _(g):
-        @pl.when(g + 2 < NC)
-        def _():
-            produce_step(g + 2)
-
-        @pl.when((g + 2 >= NC) & (g + 2 < 2 * NC))
-        def _():
-            produce_track(g + 2 - NC)
+        ahead = (g + 4) // 2
+
+        @pl.when((lax.rem(g, 2) == 0) & (ahead < NC // 2))
+        def _():
+            produce(0, ahead)
+
+        @pl.when((lax.rem(g, 2) == 0) & (ahead >= NC // 2) & (ahead < NC))
+        def _():
+            produce(1, ahead - NC // 2)
 
         @pl.when(g + 2 < 2 * NC)
         def _():
@@ -530,6 +598,15 @@
         @pl.when(g < 2 * NC)
         def _():
             z_send(g)
+
+        for lag, tangent_step in enumerate(tangent_steps):
+            @pl.when((g >= lag) & (g < lag + 4))
+            def _(lag=lag, tangent_step=tangent_step):
+                tangent_step(g - lag)
+
+        @pl.when(g == len(tangent_steps) + 3)
+        def _():
+            tangent_gates()
 
         @pl.when((g >= 2) & (g < NC + 2))
         def _():
@@ -545,17 +622,26 @@
     down_gather.drain()
     target_copy.wait_send()
 
-    @pl.loop(0, 8)
-    def _(j):
-        tk_pass(j).wait_send()
+    for a in range(2):
+        for b in range(4):
+            tk_pass(a, b).wait_send()
+            if a or b:
+                tk_copy(a, b).wait_send()
 
     @pl.loop(1, 8)
     def _(j):
-        tk_copy(j).wait_send()
         for s in range(4):
-            for p in range(2):
-                rs_copy(s, p, j).wait_send()
-                ag_copy(s, p, j).wait_send()
+            rs_copy(s, 0, j).wait_send()
+            ag_copy(s, 0, j).wait_send()
+
+    @pl.loop(0, 4)
+    def _(s):
+        pair_copy(s).wait_send()
+        t_copy(s, 1, 0).wait_send()
+        for b in range(1, 4):
+            y_copy(s, b).wait_send()
+            for a in range(2):
+                t_copy(s, a, b).wait_send()
 
     for s in range(4):
         for p in range(2):
@@ -576,9 +662,10 @@
     hbm = pl.BlockSpec(memory_space=pl.ANY)
     smem = pl.BlockSpec(memory_space=pltpu.SMEM)
     dma = pltpu.SemaphoreType.DMA
-    weight = jax.ShapeDtypeStruct((D, COLS), bf16)
+    weight = jax.ShapeDtypeStruct((COLS, D), bf16)
     wide = pltpu.VMEM((TOK, COLS), f32)
-    mixed = pltpu.VMEM((2 * NC, PK, 128), bf16)
+    turned = pltpu.VMEM((COLS, TOK), f32)
+    mixed = pltpu.VMEM((2 * NC, COLS, CH), bf16)
     gather_sems = [dma((2,))] * 4 + [dma((4, 2))] * 4
     mixed_weights, mixed_tracker = pl.pallas_call(
         kernel,
@@ -586,30 +673,31 @@
         in_specs=[vmem, vmem, hbm, hbm, hbm, vmem, vmem, smem, smem],
         out_specs=(hbm, hbm),
         scratch_shapes=[
-            pltpu.VMEM((D, COLS), bf16),
-            pltpu.VMEM((D, COLS), bf16),
-            pltpu.VMEM((D, COLS), bf16),
+            pltpu.VMEM((COLS, D), bf16),
+            pltpu.VMEM((COLS, D), bf16),
+            pltpu.VMEM((COLS, D), bf16),
             pltpu.VMEM((16, 48, 1024), bf16),
             pltpu.VMEM((2, 48, 1024), bf16),
             pltpu.VMEM((TOK, D), bf16),
-            pltpu.VMEM((D, TOK), bf16),
-            pltpu.VMEM((4, 4, 128, COLS), bf16),
-            pltpu.VMEM((4, COLS, 512), bf16),
-            wide, wide, wide, wide, wide,
+            pltpu.VMEM((4, 4, COLS, 128), bf16),
+            pltpu.VMEM((4, 4, COLS, 128), bf16),
+            wide, wide, wide, turned, turned, turned, turned,
             pltpu.VMEM((2, TOK, COLS), bf16),
-            pltpu.VMEM((2, TOK, COLS), bf16),
+            pltpu.VMEM((2, COLS, TOK), bf16),
             pltpu.VMEM((2, 4, TOK, 256), bf16),
             pltpu.VMEM((2, 4, TOK, 256), bf16),
             pltpu.VMEM((2, 4, TOK, 256), f32),
-            pltpu.VMEM((2, 4, TOK, 256), bf16),
+            pltpu.VMEM((2, 4, 2, TOK // 2, 256), bf16),
             pltpu.VMEM((2, 4, 8, 48, 256), bf16),
+            pltpu.VMEM((4, 48, 256), bf16),
+            pltpu.VMEM((4, 48, 256), bf16),
             pltpu.VMEM((2, 4, 2, TOK, 256), bf16),
             mixed, mixed, mixed, mixed, mixed, mixed,
-            pltpu.VMEM((4, PK, 128), f32),
-            pltpu.VMEM((2, CH, COLS), bf16),
+            pltpu.VMEM((4, COLS, CH), f32),
+            pltpu.VMEM((2, COLS, CH), bf16),
             dma((3,)), dma((8,)), dma((16,)), dma((8,)), dma, dma,
             *gather_sems, *gather_sems,
-            dma((2, 4)), dma((2, 4)), dma((2, 4, 8)), dma((2, 4, 8)),
+            dma((2, 4)), dma((2, 4)), dma((2, 4, 8)), dma((2, 4, 8)), dma((4,)), dma((4,)),
             dma((2, 4, 8)), dma((2, 4, 8)), dma((2, 4)), dma((2, 4)),
             dma((2 * NC, 2)), dma((2 * NC, 2)), dma((2 * NC, 2)), dma((2 * NC, 2)),
             dma((2 * NC, 2)), dma((2 * NC, 2)), dma((2,)),
@@ -619,10 +707,10 @@
         ),
         name="step_and_mix",
     )(
-        tokens[0], targets[0], gate_weight[0], probes[0], tracker[0], up_weight, down_weight,
-        neighbours, numerators,
+        tokens[0], targets[0], gate_weight[0].T, probes[0].T, tracker[0].T, up_weight.T, down_weight,
+        neighbours.T, numerators.T,
     )
-    return (mixed_weights[None], mixed_tracker[None])
+    return (mixed_weights.T[None], mixed_tracker.T[None])
 
 
 def solution(mesh):

time: 295 us -> 260 us (0.88)
  local copies, waits for them, and re-layouts: 20.9 us -> 4.3 us
  Pallas kernels: 271 us -> 255 us
    unnamed x12 -> x4, local copies, waits for them, and re-layouts: 20.9 us -> 4.3 us
    pallas_call x1, Pallas kernels: 271 us -> 255 us  [local(): pl.pallas_call(kernel, out_shape=(weight, weight), in_specs=[vmem, vmem,...]
where the time goes in v2:
time: 260 us
  Pallas kernels  255 us (98%)
  local copies, waits for them, and re-layouts  4.3 us (2%)
    pallas_call x1, Pallas kernels, local(): pl.pallas_call(kernel, out_shape=(weight, weight), in_specs=[vmem, vmem,...  255 us

profile of v2, /device:TPU:16, one launch (start us, length us, event | category | flops | bytes accessed | tf_op | source)
XLA Modules:
  0.0 259.6 jit_solution(5093492925831336198)
XLA Ops:
  0.6 254.7 %step_and_mix.1 = (bf16[448,2048]{1,0:T(8,128)(2,1)}, bf16[448,2048]{1,0:T(8,128)(2,1)}) custom-call(bf16[24,2048]{1,0:T(8,128)(2,1)} %bitcast.26, bf16[24,2048]{1,0:T(8,128)(2,1)} %bitcast.27, bf16[448,2048]{1,0:T(8,128)(2,1)} %bitcast.22, bf16[448,2048]{1,0:T(8,128)(2,1)} %bitcast.23, bf16[448,2048]{1,0:T(8,128)(2,1)} %bitcast.24, ...), custom_call_target="tpu_custom_call" | custom-call | tf_op jit(solution)/shard_map/step_and_mix/pallas_call | solution.py:670
  255.3 0.0 copy-start
  255.3 3.1 %copy.13 = bf16[1,2048,448]{1,2,0:T(8,128)(2,1)} copy(bf16[1,2048,448]{1,2,0:T(8,128)(2,1)} %bitcast.21) | data formatting | bytes 3670016
  258.4 0.0 copy-done
  258.4 1.2 copy.14
Async XLA Ops:
  255.3 3.1 %copy-start = (bf16[448,2048]{1,0:T(8,128)(2,1)S(1)}, bf16[448,2048]{1,0:T(8,128)(2,1)}, u32[]{:S(2)}) copy-start(bf16[448,2048]{1,0:T(8,128)(2,1)} %get-tuple-element.5) | copy-start | bytes 5505028

commit v3 on v2

--- a/solution.py
+++ b/solution.py
@@ -23,6 +23,7 @@
 CH = 128
 NC = D // CH
 HALF = COLS // 2
+RING = 8
 f32 = jnp.float32
 bf16 = jnp.bfloat16
 
@@ -32,9 +33,9 @@
 
 
 class Gather:
-    def __init__(self, slot, rows, own, sems, zh, x, device):
-        self.slot, self.rows, self.own = slot, rows, own
-        (self.z_s, self.z_r, self.zf_s, self.zf_r, self.x_s, self.x_r, self.xf_s, self.xf_r) = sems
+    def __init__(self, ref, rows, own, sems, zh, x, device):
+        self.ref, self.slot, self.rows, self.own = ref, lambda column, row: ref.at[row, column], rows, own
+        (self.sent, self.z_r, self.zf_r, self.x_r, self.xf_r) = sems
         self.zh, self.x, self.device = zh, x, device
 
     def part(self, ref, half):
@@ -43,7 +44,7 @@
 
     def z_copy(self, way):
         return pltpu.make_async_remote_copy(
-            self.own, self.slot(self.x, self.zh), self.z_s.at[way], self.z_r.at[way],
+            self.own, self.slot(self.x, self.zh), self.sent.at[0], self.z_r.at[way],
             device_id=self.device(1 - 2 * way, 0), device_id_type=MESH)
 
     def z_start(self):
@@ -53,7 +54,7 @@
     def z_forward_copy(self, way):
         block = self.part(self.slot(self.x, mod(self.zh - (1 - 2 * way), 4)), way)
         return pltpu.make_async_remote_copy(
-            block, block, self.zf_s.at[way], self.zf_r.at[way],
+            block, block, self.sent.at[0], self.zf_r,
             device_id=self.device(1 - 2 * way, 0), device_id_type=MESH)
 
     def z_forward(self):
@@ -61,14 +62,17 @@
             self.z_copy(way).wait_recv()
             self.z_forward_copy(way).start()
 
+    def whole(self, block, send, recv):
+        return pltpu.make_async_remote_copy(
+            block, block, send, recv, device_id=self.device(1, 0), device_id_type=MESH)
+
     def z_last(self):
-        for way in range(2):
-            self.z_forward_copy(way).wait_recv()
+        self.whole(self.slot(self.x, mod(self.zh + 2, 4)), self.sent.at[0], self.zf_r).wait_recv()
 
     def x_copy(self, q, way):
         block = self.slot(self.x, mod(self.zh + q, 4))
         return pltpu.make_async_remote_copy(
-            self.own if q == 0 else block, block, self.x_s.at[q, way], self.x_r.at[q, way],
+            self.own if q == 0 else block, block, self.sent.at[1], self.x_r.at[q, way],
             device_id=self.device(0, 1 - 2 * way), device_id_type=MESH)
 
     def x_start(self, q):
@@ -78,7 +82,7 @@
     def x_forward_copy(self, q, way):
         block = self.part(self.slot(mod(self.x - (1 - 2 * way), 4), mod(self.zh + q, 4)), way)
         return pltpu.make_async_remote_copy(
-            block, block, self.xf_s.at[q, way], self.xf_r.at[q, way],
+            block, block, self.sent.at[2], self.xf_r.at[q],
             device_id=self.device(0, 1 - 2 * way), device_id_type=MESH)
 
     def x_forward(self, q):
@@ -87,29 +91,26 @@
             self.x_forward_copy(q, way).start()
 
     def x_last(self, q):
-        for way in range(2):
-            self.x_forward_copy(q, way).wait_recv()
+        block = self.slot(mod(self.x + 2, 4), mod(self.zh + q, 4))
+        self.whole(block, self.sent.at[2], self.xf_r.at[q]).wait_recv()
 
     def drain(self):
-        for way in range(2):
-            self.z_copy(way).wait_send()
-            self.z_forward_copy(way).wait_send()
-            for q in range(4):
-                self.x_copy(q, way).wait_send()
-                self.x_forward_copy(q, way).wait_send()
+        for i, blocks in enumerate((self.ref.at[0, pl.ds(0, 3)], self.ref.at[pl.ds(0, 2)], self.ref.at[0])):
+            self.whole(blocks, self.sent.at[i], self.zf_r).wait_send()
 
 
 def kernel(
-    tok_ref, tgt_ref, w_hbm, p_hbm, h_hbm, up_ref, down_ref, nb_ref, num_ref,
+    tok_ref, tgt_ref, w_hbm, p_hbm, h_hbm, up_ref, down_ref, nb_hbm, num_hbm,
     out_w, out_t,
+    nb_ref, num_ref,
     w_ref, p_ref, h_ref, tk, pair, x_all, upb, dnb,
     gate_acc, probe_acc, up_acc, first_turned, second_turned, grad_acc, tang_acc,
     hid, gates, core_send, core_recv, own_part, rs_send, rs_recv, pair_send, pair_recv, res,
     own_mix, left_mix, right_mix, far_mix, below, above, mine, staged,
-    load_sem, tk_s, tk_r, tkf_s, tg_s, tg_r,
-    uz_s, uz_r, uzf_s, uzf_r, ux_s, ux_r, uxf_s, uxf_r,
-    dz_s, dz_r, dzf_s, dzf_r, dx_s, dx_r, dxf_s, dxf_r,
-    cs_s, cs_r, rs_s, rs_r, pair_s, pair_r, ag_s, ag_r, ac_s, ac_r,
+    load_sem, tk_s, tk_r, tg_s, tg_r,
+    u_s, uz_r, uzf_r, ux_r, uxf_r,
+    d_s, dz_r, dzf_r, dx_r, dxf_r,
+    cs_s, cs_r, rs_s, rs_r, pair_s, pair_r, ag_s, ag_r, agp_r, ac_s, ac_r,
     mx_s, mx_r, mf_s, mf_r, mz_s, mz_r, out_sem,
 ):
     r = lax.axis_index("replica")
@@ -138,13 +139,6 @@
         return pltpu.make_async_remote_copy(
             src, dst, send, recv, device_id=where, device_id_type=MESH)
 
-    loads = [
-        pltpu.make_async_copy(src, dst, load_sem.at[i])
-        for i, (src, dst) in enumerate(((w_hbm, w_ref), (p_hbm, p_ref), (h_hbm, h_ref)))
-    ]
-    for load in loads:
-        load.start()
-
     barrier = pltpu.get_barrier_semaphore()
     partners = [device(1, 0), device(-1, 0), device(0, 1), device(0, -1), sibling]
     for where in partners:
@@ -154,14 +148,22 @@
     def _(j):
         pl.semaphore_signal(barrier, inc=1, device_id=peer(j), device_id_type=MESH)
 
+    locals_in = (
+        (up_ref, upb.at[zh, x]), (down_ref, dnb.at[zh, x]), (w_hbm, w_ref), (p_hbm, p_ref),
+        (h_hbm, h_ref), (nb_hbm, nb_ref), (num_hbm, num_ref),
+    )
+    loads = [
+        pltpu.make_async_copy(src, dst, load_sem.at[i]) for i, (src, dst) in enumerate(locals_in)
+    ]
+    for load in loads:
+        load.start()
+
     def packed_rows(ref):
         block = ref[...].astype(f32)
         return jnp.concatenate([block[:, :1024], block[:, 1024:]], axis=0).astype(bf16)
 
     tk[t] = packed_rows(tok_ref)
     pair[core] = packed_rows(tgt_ref)
-    upb[x, zh] = up_ref[...]
-    dnb[x, zh] = down_ref[...]
     pl.semaphore_wait(barrier, 12)
 
     def tk_slot(a, b):
@@ -170,23 +172,19 @@
     def tk_copy(a, b):
         block = tk_slot(a, 0) if b else tk_slot(0, 0)
         where = same_core(0, b) if b else same_core(1, 0)
-        return remote(block, block, tk_s.at[4 * a + b], tk_r.at[4 * a + b], where)
+        return remote(block, block, tk_s.at[0], tk_r.at[2 * a + (b > 0)], where)
 
     def tk_pass(a, b):
         block = tk_slot(a, -b)
-        return remote(block, block, tkf_s.at[4 * a + b], tk_r.at[8 + 4 * a + b], sibling)
+        return remote(block, block, tk_s.at[1], tk_r.at[0], sibling)
+
+    def tk_wait(count, send, recv):
+        return remote(tk.at[pl.ds(0, count)], tk.at[pl.ds(0, count)], tk_s.at[send], tk_r.at[recv], sibling)
 
     target_copy = remote(pair.at[core], pair.at[core], tg_s, tg_r, sibling)
 
-    def slots(ref):
-        return lambda column, row: ref.at[column, row]
-
-    up_gather = Gather(
-        slots(upb), COLS, up_ref,
-        (uz_s, uz_r, uzf_s, uzf_r, ux_s, ux_r, uxf_s, uxf_r), zh, x, device)
-    down_gather = Gather(
-        slots(dnb), COLS, down_ref,
-        (dz_s, dz_r, dzf_s, dzf_r, dx_s, dx_r, dxf_s, dxf_r), zh, x, device)
+    up_gather = Gather(upb, COLS, up_ref, (u_s, uz_r, uzf_r, ux_r, uxf_r), zh, x, device)
+    down_gather = Gather(dnb, COLS, down_ref, (d_s, dz_r, dzf_r, dx_r, dxf_r), zh, x, device)
 
     tk_copy(1, 0).start()
     for b in range(1, 4):
@@ -200,28 +198,23 @@
     for b in range(1, 4):
         tk_copy(1, b).start()
     tk_pass(1, 0).start()
+    down_gather.x_start(0)
+    up_gather.x_forward(0)
     up_gather.z_forward()
     up_gather.x_start(1)
     up_gather.x_start(3)
     down_gather.z_start()
-    up_gather.x_forward(0)
+    tk_wait(3, 0, 1).wait_recv()
     for b in range(1, 4):
-        tk_copy(0, b).wait_recv()
         tk_pass(0, b).start()
+    down_gather.x_forward(0)
     up_gather.z_last()
     up_gather.x_start(2)
-    down_gather.x_start(0)
+    tk_wait(3, 0, 3).wait_recv()
+    for b in range(1, 4):
+        tk_pass(1, b).start()
     up_gather.x_forward(1)
-    up_gather.x_forward(3)
-    for b in range(1, 4):
-        tk_copy(1, b).wait_recv()
-        tk_pass(1, b).start()
-    down_gather.z_forward()
-    down_gather.x_start(1)
-    down_gather.x_start(3)
-    for a in range(2):
-        for b in range(4):
-            tk_pass(a, b).wait_recv()
+    tk_wait(8, 1, 0).wait_recv()
 
     @pl.loop(0, 8)
     def _(c):
@@ -229,10 +222,13 @@
         rows = [jnp.concatenate([b[:24], b[24:]], axis=1) for b in blocks]
         x_all[pl.ds(pl.multiple_of(c * 48, 48), 48), :] = jnp.concatenate(rows, axis=0).astype(bf16)
 
-    up_gather.x_forward(2)
-
-    def joined(ref, column, first, count):
-        return jnp.concatenate([ref[column, first + i] for i in range(count)], axis=1)
+    up_gather.x_forward(3)
+    down_gather.z_forward()
+    down_gather.x_start(1)
+    down_gather.x_start(3)
+
+    def joined(ref, row, first, count):
+        return jnp.concatenate([ref[row, first + i] for i in range(count)], axis=1)
 
     def rows_dot(left, right):
         return lax.dot_general(left, right, (((1,), (1,)), ((), ())), preferred_element_type=f32)
@@ -240,29 +236,25 @@
     def wide_dot(acc, weight):
         acc[...] = rows_dot(x_all[...], weight[...])
 
-    loads[0].wait()
+    loads[2].wait()
     wide_dot(gate_acc, w_ref)
+    up_gather.x_forward(2)
+    loads[3].wait()
+    wide_dot(probe_acc, p_ref)
     down_gather.z_last()
     down_gather.x_start(2)
-    down_gather.x_forward(0)
+    loads[0].wait()
     loads[1].wait()
-    wide_dot(probe_acc, p_ref)
-
-    for q in range(4):
+
+    def up_rows(q):
+        row = mod(zh + q, 4)
+        return rows_dot(x_all[:, pl.ds(pl.multiple_of(512 * row, 512), 512)], joined(upb, row, 0, 4))
+
+    for q in (0, 1, 3):
         up_gather.x_last(q)
-
-    @pl.loop(0, 4)
-    def _(column):
-        lanes = [x_all[:, pl.ds(pl.multiple_of(512 * z + 128 * column, 128), 128)] for z in range(4)]
-        part = rows_dot(jnp.concatenate(lanes, axis=1), joined(upb, column, 0, 4))
-
-        @pl.when(column == 0)
-        def _():
-            up_acc[...] = part
-
-        @pl.when(column > 0)
-        def _():
-            up_acc[...] += part
+    up_acc[...] = up_rows(0) + up_rows(1) + up_rows(3)
+    up_gather.x_last(2)
+    up_acc[...] += up_rows(2)
 
     @pl.loop(0, 8)
     def _(c):
@@ -279,19 +271,15 @@
         gate_acc[rows, :] = first
         probe_acc[rows, :] = up_pre * slope_two * probe_pre
 
-    down_gather.x_forward(1)
-    down_gather.x_forward(3)
-
     target_copy.wait_recv()
-    down_gather.x_forward(2)
-
-    columns = [mod(x + step, 4) for step in (0, 3, 1, 2)]
+
+    order = (0, 1, 3, 2)
 
     def column(s, p):
-        return columns[s] if p == 0 else lax.rem(x + s, 4)
+        return mod(zh + order[s], 4) if p == 0 else lax.rem(zh + s, 4)
 
     def core_copy(s, p):
-        return remote(core_send.at[p, s], core_recv.at[p, s], cs_s.at[p, s], cs_r.at[p, s], sibling)
+        return remote(core_send.at[p, s], core_recv.at[p, s], cs_s, cs_r.at[p, s], sibling)
 
     def forward(s, p):
         away = jnp.dot(hid[p], joined(dnb, column(s, p), 2 * (1 - core), 2), preferred_element_type=f32)
@@ -300,11 +288,14 @@
         here = jnp.dot(hid[p], joined(dnb, column(s, p), 2 * core, 2), preferred_element_type=f32)
         own_part[p, s] = here * INV_HIDDEN
 
+    def blocks_wait(blocks, send, recv):
+        return remote(blocks, blocks, send, recv, sibling)
+
     def rs_copy(s, p, j):
         to = lax.rem(chip + j, 8)
         return remote(
             rs_send.at[p, s, to // 4, pl.ds(pl.multiple_of(48 * lax.rem(to, 4), 48), 48)], rs_recv.at[p, s, j],
-            rs_s.at[p, s, j], rs_r.at[p, s, j], peer(j))
+            rs_s.at[p], rs_r.at[p, s], peer(j))
 
     def core_sum(s, p):
         core_copy(s, p).wait_recv()
@@ -323,24 +314,19 @@
 
     def ag_copy(s, p, j):
         block = res.at[p, s, core, own_rows]
-        return remote(block, block, ag_s.at[p, s, j], ag_r.at[p, s, j], peer(j))
+        return remote(block, block, ag_s.at[p], ag_r.at[p, s], peer(j))
 
     def reduce(s, p):
-        @pl.loop(1, 8)
-        def _(j):
-            rs_copy(s, p, j).wait_recv()
-
+        blocks_wait(rs_recv.at[p, s, pl.ds(1, 7)], rs_s.at[p], rs_r.at[p, s]).wait_recv()
         total = own_part[p, s, own_rows, :]
         for j in range(1, 8):
             total = total + rs_recv[p, s, j].astype(f32)
+        row = column(s, p)
+        at = pl.ds(pl.multiple_of(512 * lax.rem(row, 2) + 256 * core, 256), 256)
         target = []
         for k in range(2):
-            pieces = []
-            for m in range(2):
-                at = pl.ds(pl.multiple_of(512 * m + 128 * columns[s], 128), 128)
-                top = pair[k, :, at].astype(f32)
-                pieces.append(jnp.where(core == 0, top[:24], top[24:]))
-            target.append(jnp.concatenate(pieces, axis=1))
+            both = pair[k, :, at].astype(f32)
+            target.append(jnp.where(row < 2, both[:24], both[24:]))
         total = total - jnp.concatenate(target, axis=0)
         res[p, s, core, own_rows, :] = total.astype(bf16)
 
@@ -349,13 +335,10 @@
             ag_copy(s, p, j).start()
 
     def across_copy(s, p, k):
-        return remote(res.at[p, s, k], res.at[p, s, k], ac_s.at[p, s], ac_r.at[p, s], sibling)
+        return remote(res.at[p, s, k], res.at[p, s, k], ac_s, ac_r.at[p, s], sibling)
 
     def across(s, p):
-        @pl.loop(1, 8)
-        def _(j):
-            ag_copy(s, p, j).wait_recv()
-
+        blocks_wait(rs_recv.at[p, s, pl.ds(1, 7)], ag_s.at[p], ag_r.at[p, s]).wait_recv()
         across_copy(s, p, core).start()
 
     def backward(s, p, acc):
@@ -371,10 +354,10 @@
         rows = pl.ds(pl.multiple_of(48 * mod(y + b, 4), 48), 48)
         return remote(
             rs_send.at[1, s, :, rows], rs_recv.at[1, s, pl.ds(2 * b, 2)],
-            rs_s.at[1, s, b], rs_r.at[1, s, b], same_core(0, b))
+            rs_s.at[1], rs_r.at[1, s], same_core(0, b))
 
     def pair_copy(s):
-        return remote(pair_send.at[s], pair_recv.at[s], pair_s.at[s], pair_r.at[s], same_core(1, 0))
+        return remote(pair_send.at[s], pair_recv.at[s], pair_s, pair_r.at[s], same_core(1, 0))
 
     def y_scatter(s):
         core_sum(s, 1)
@@ -382,8 +365,7 @@
             y_copy(s, b).start()
 
     def y_reduce(s):
-        for b in range(1, 4):
-            y_copy(s, b).wait_recv()
+        blocks_wait(rs_recv.at[1, s, pl.ds(2, 6)], rs_s.at[1], rs_r.at[1, s]).wait_recv()
 
         def total(at):
             value = own_part[1, s, pl.ds(pl.multiple_of(48 * (4 * at + y), 48), 48), :]
@@ -399,7 +381,7 @@
         at = chip_at(a, 0) if b else chip
         block = res.at[1, s, core, pl.ds(pl.multiple_of(48 * at, 48), 48)]
         where = same_core(0, b) if b else same_core(1, 0)
-        return remote(block, block, ag_s.at[1, s, 4 * a + b], ag_r.at[1, s, 4 * a + b], where)
+        return remote(block, block, ag_s.at[1], ag_r.at[1, s] if b else agp_r.at[s], where)
 
     def pair_reduce(s):
         pair_copy(s).wait_recv()
@@ -415,9 +397,7 @@
             t_copy(s, 1, b).start()
 
     def t_across(s):
-        for a in range(2):
-            for b in range(1, 4):
-                t_copy(s, a, b).wait_recv()
+        blocks_wait(rs_recv.at[1, s, pl.ds(2, 6)], ag_s.at[1], ag_r.at[1, s]).wait_recv()
         across_copy(s, 1, core).start()
 
     def turn(p):
@@ -429,14 +409,17 @@
             turned[:, tokens_at] = source[tokens_at, :].T
 
     def ready(s):
-        if s == 3:
-            for q in range(4):
-                down_gather.x_last(q)
+        down_gather.x_last(order[s])
+
+    def passed_on(step):
+        if step < 3:
+            down_gather.x_forward(order[step + 1])
 
     for step in range(8):
         if step < 4:
             ready(step)
             forward(step, 0)
+            passed_on(step)
         if 0 <= step - 1 < 4:
             scatter(step - 1, 0)
         if step in (4, 5):
@@ -448,7 +431,7 @@
         if 0 <= step - 4 < 4:
             backward(step - 4, 0, grad_acc)
 
-    loads[2].wait()
+    loads[4].wait()
     tang_acc[...] = jnp.zeros_like(tang_acc)
 
     @pl.loop(0, 7)
@@ -486,6 +469,8 @@
             total = total + num_ref[k, r]
         return (DEN - total).astype(f32) * (1.0 / DEN)
 
+    loads[5].wait()
+    loads[6].wait()
     sources = [replica_at(0, dx) for dx in (0, -1, 1, 2)]
     here_c = [self_share()] + [share(r, source) for source in sources[1:]]
     up_c = [share(replica_at(1, 0), source) for source in sources]
@@ -506,20 +491,25 @@
     def mx_copy(g, way):
         return remote(
             own_mix.at[g], (left_mix if way == 0 else right_mix).at[g],
-            mx_s.at[g, way], mx_r.at[g, way], device(0, 1 - 2 * way))
+            mx_s.at[lax.rem(g, RING), way], mx_r.at[lax.rem(g, RING), way], device(0, 1 - 2 * way))
 
     def mf_copy(g, way):
         part = pl.ds(way * HALF, HALF)
         return remote(
             (left_mix if way == 0 else right_mix).at[g, part], far_mix.at[g, part],
-            mf_s.at[g, way], mf_r.at[g, way], device(0, 1 - 2 * way))
+            mf_s.at[lax.rem(g, RING), way], mf_r.at[lax.rem(g, RING), way], device(0, 1 - 2 * way))
 
     def mz_copy(g, way):
         return remote(
             (left_mix if way == 0 else right_mix).at[g], (below if way == 0 else above).at[g],
-            mz_s.at[g, way], mz_r.at[g, way], device(1 - 2 * way, 0))
+            mz_s.at[lax.rem(g, RING), way], mz_r.at[lax.rem(g, RING), way], device(1 - 2 * way, 0))
 
     def x_send(g):
+        @pl.when(g >= RING)
+        def _():
+            for way in range(2):
+                mx_copy(g - RING, way).wait_send()
+
         for way in range(2):
             mx_copy(g, way).start()
 
@@ -549,6 +539,11 @@
             left_mix[g, rows, :] = weighted(up_c).astype(bf16)
             right_mix[g, rows, :] = weighted(down_c).astype(bf16)
 
+        @pl.when(g >= RING)
+        def _():
+            for way in range(2):
+                mz_copy(g - RING, way).wait_send()
+
         for way in range(2):
             mz_copy(g, way).start()
 
@@ -571,8 +566,8 @@
 
     produce(0, 0)
     x_send(0)
+    produce(0, 1)
     x_send(1)
-    produce(0, 1)
     x_pass(0)
 
     @pl.loop(0, 2 * NC + 2)
@@ -622,34 +617,17 @@
     down_gather.drain()
     target_copy.wait_send()
 
-    for a in range(2):
-        for b in range(4):
-            tk_pass(a, b).wait_send()
-            if a or b:
-                tk_copy(a, b).wait_send()
-
-    @pl.loop(1, 8)
-    def _(j):
-        for s in range(4):
-            rs_copy(s, 0, j).wait_send()
-            ag_copy(s, 0, j).wait_send()
-
-    @pl.loop(0, 4)
-    def _(s):
-        pair_copy(s).wait_send()
-        t_copy(s, 1, 0).wait_send()
-        for b in range(1, 4):
-            y_copy(s, b).wait_send()
-            for a in range(2):
-                t_copy(s, a, b).wait_send()
-
-    for s in range(4):
-        for p in range(2):
-            core_copy(s, p).wait_send()
-            across_copy(s, p, core).wait_send()
-
-    @pl.loop(0, 2 * NC)
-    def _(g):
+    tk_wait(7, 0, 0).wait_send()
+    tk_wait(8, 1, 0).wait_send()
+
+    blocks_wait(rs_recv.at[0, :, pl.ds(0, 7)], rs_s.at[0], rs_r.at[0, 0]).wait_send()
+    blocks_wait(rs_recv.at[0, :, pl.ds(0, 7)], ag_s.at[0], ag_r.at[0, 0]).wait_send()
+    blocks_wait(rs_recv.at[1, :, pl.ds(0, 6)], rs_s.at[1], rs_r.at[1, 0]).wait_send()
+    blocks_wait(rs_recv.at[1, :, pl.ds(0, 7)], ag_s.at[1], ag_r.at[1, 0]).wait_send()
+    blocks_wait(pair_send, pair_s, pair_r.at[0]).wait_send()
+    blocks_wait(core_send, cs_s, cs_r.at[0, 0]).wait_send()
+    blocks_wait(core_send, ac_s, ac_r.at[0, 0]).wait_send()
+    for g in range(2 * NC - RING, 2 * NC):
         for way in range(2):
             mx_copy(g, way).wait_send()
             mz_copy(g, way).wait_send()
@@ -660,19 +638,20 @@
 ):
     vmem = pl.BlockSpec(memory_space=pltpu.VMEM)
     hbm = pl.BlockSpec(memory_space=pl.ANY)
-    smem = pl.BlockSpec(memory_space=pltpu.SMEM)
     dma = pltpu.SemaphoreType.DMA
     weight = jax.ShapeDtypeStruct((COLS, D), bf16)
     wide = pltpu.VMEM((TOK, COLS), f32)
     turned = pltpu.VMEM((COLS, TOK), f32)
     mixed = pltpu.VMEM((2 * NC, COLS, CH), bf16)
-    gather_sems = [dma((2,))] * 4 + [dma((4, 2))] * 4
+    gather_sems = [dma((3,)), dma((2,)), dma, dma((4, 2)), dma((4,))]
     mixed_weights, mixed_tracker = pl.pallas_call(
         kernel,
         out_shape=(weight, weight),
-        in_specs=[vmem, vmem, hbm, hbm, hbm, vmem, vmem, smem, smem],
+        in_specs=[vmem, vmem, hbm, hbm, hbm, hbm, hbm, hbm, hbm],
         out_specs=(hbm, hbm),
         scratch_shapes=[
+            pltpu.SMEM((6, 16), jnp.int32),
+            pltpu.SMEM((6, 16), jnp.int32),
             pltpu.VMEM((COLS, D), bf16),
             pltpu.VMEM((COLS, D), bf16),
             pltpu.VMEM((COLS, D), bf16),
@@ -695,12 +674,12 @@
             mixed, mixed, mixed, mixed, mixed, mixed,
             pltpu.VMEM((4, COLS, CH), f32),
             pltpu.VMEM((2, COLS, CH), bf16),
-            dma((3,)), dma((8,)), dma((16,)), dma((8,)), dma, dma,
+            dma((7,)), dma((2,)), dma((4,)), dma, dma,
             *gather_sems, *gather_sems,
-            dma((2, 4)), dma((2, 4)), dma((2, 4, 8)), dma((2, 4, 8)), dma((4,)), dma((4,)),
-            dma((2, 4, 8)), dma((2, 4, 8)), dma((2, 4)), dma((2, 4)),
-            dma((2 * NC, 2)), dma((2 * NC, 2)), dma((2 * NC, 2)), dma((2 * NC, 2)),
-            dma((2 * NC, 2)), dma((2 * NC, 2)), dma((2,)),
+            dma, dma((2, 4)), dma((2,)), dma((2, 4)), dma, dma((4,)),
+            dma((2,)), dma((2, 4)), dma((4,)), dma, dma((2, 4)),
+            dma((RING, 2)), dma((RING, 2)), dma((RING, 2)), dma((RING, 2)),
+            dma((RING, 2)), dma((RING, 2)), dma((2,)),
         ],
         compiler_params=pltpu.CompilerParams(
             collective_id=0, has_side_effects=True, vmem_limit_bytes=63 << 20

time: 260 us -> 254 us (0.977)
  Pallas kernels: 255 us -> 248 us
    pallas_call x1, Pallas kernels: 255 us -> 248 us  [local(): pl.pallas_call(kernel, out_shape=(weight, weight), in_specs=[vmem, vmem,...]
where the time goes in v3:
time: 254 us; the launch traced here: 253 us
  Pallas kernels  248 us (98%)
  local copies, waits for them, and re-layouts  4.3 us (2%)
    pallas_call x1, Pallas kernels, local(): pl.pallas_call(kernel, out_shape=(weight, weight), in_specs=[vmem, vmem,...  248 us

profile of v3, /device:TPU:16, one launch (start us, length us, event | category | flops | bytes accessed | tf_op | source)
XLA Modules:
  0.0 252.9 jit_solution(12986786397209891448)
XLA Ops:
  0.6 247.9 %step_and_mix.1 = (bf16[448,2048]{1,0:T(8,128)(2,1)}, bf16[448,2048]{1,0:T(8,128)(2,1)}) custom-call(bf16[24,2048]{1,0:T(8,128)(2,1)} %bitcast.26, bf16[24,2048]{1,0:T(8,128)(2,1)} %bitcast.27, bf16[448,2048]{1,0:T(8,128)(2,1)} %bitcast.22, bf16[448,2048]{1,0:T(8,128)(2,1)} %bitcast.23, bf16[448,2048]{1,0:T(8,128)(2,1)} %bitcast.24, ...), custom_call_target="tpu_custom_call" | custom-call | tf_op jit(solution)/shard_map/step_and_mix/pallas_call | solution.py:647
  248.6 0.0 copy-start
  248.6 3.1 %copy.13 = bf16[1,2048,448]{1,2,0:T(8,128)(2,1)} copy(bf16[1,2048,448]{1,2,0:T(8,128)(2,1)} %bitcast.21) | data formatting | bytes 3670016
  251.6 0.0 copy-done
  251.6 1.2 copy.14
Async XLA Ops:
  248.6 3.1 %copy-start = (bf16[448,2048]{1,0:T(8,128)(2,1)S(1)}, bf16[448,2048]{1,0:T(8,128)(2,1)}, u32[]{:S(2)}) copy-start(bf16[448,2048]{1,0:T(8,128)(2,1)} %get-tuple-element.5) | copy-start | bytes 5505028

commit v4 on v3

--- a/solution.py
+++ b/solution.py
@@ -23,6 +23,7 @@
 CH = 128
 NC = D // CH
 HALF = COLS // 2
+FIRST_Z = 352
 RING = 8
 f32 = jnp.float32
 bf16 = jnp.bfloat16
@@ -33,70 +34,104 @@
 
 
 class Gather:
-    def __init__(self, ref, rows, own, sems, zh, x, device):
-        self.ref, self.slot, self.rows, self.own = ref, lambda column, row: ref.at[row, column], rows, own
+    first, rows = 0, FIRST_Z
+
+    def __init__(self, ref, own, sems, zh, x, device):
+        self.ref, self.own, self.zh, self.x, self.device = ref, own.at[pl.ds(self.first, self.rows)], zh, x, device
         (self.sent, self.z_r, self.zf_r, self.x_r, self.xf_r) = sems
-        self.zh, self.x, self.device = zh, x, device
-
-    def part(self, ref, half):
+
+    def slot(self, column, row):
+        return self.ref.at[row, column, pl.ds(self.first, self.rows)]
+
+    def part(self, column, row, half):
         size = self.rows // 2
-        return ref.at[pl.ds(half * size, size)]
+        return self.ref.at[row, column, pl.ds(self.first + half * size, size)]
+
+    def copy(self, src, dst, send, recv, dz, dx):
+        return pltpu.make_async_remote_copy(
+            src, dst, self.sent.at[send], recv, device_id=self.device(dz, dx), device_id_type=MESH)
 
     def z_copy(self, way):
-        return pltpu.make_async_remote_copy(
-            self.own, self.slot(self.x, self.zh), self.sent.at[0], self.z_r.at[way],
-            device_id=self.device(1 - 2 * way, 0), device_id_type=MESH)
+        return self.copy(self.own, self.slot(self.x, self.zh), 0, self.z_r.at[way], 1 - 2 * way, 0)
 
     def z_start(self):
         for way in range(2):
             self.z_copy(way).start()
 
-    def z_forward_copy(self, way):
-        block = self.part(self.slot(self.x, mod(self.zh - (1 - 2 * way), 4)), way)
-        return pltpu.make_async_remote_copy(
-            block, block, self.sent.at[0], self.zf_r,
-            device_id=self.device(1 - 2 * way, 0), device_id_type=MESH)
-
     def z_forward(self):
         for way in range(2):
             self.z_copy(way).wait_recv()
-            self.z_forward_copy(way).start()
+            block = self.part(self.x, mod(self.zh - (1 - 2 * way), 4), way)
+            self.copy(block, block, 0, self.zf_r, 1 - 2 * way, 0).start()
 
     def whole(self, block, send, recv):
-        return pltpu.make_async_remote_copy(
-            block, block, send, recv, device_id=self.device(1, 0), device_id_type=MESH)
+        return self.copy(block, block, send, recv, 1, 0)
 
     def z_last(self):
-        self.whole(self.slot(self.x, mod(self.zh + 2, 4)), self.sent.at[0], self.zf_r).wait_recv()
+        self.whole(self.slot(self.x, mod(self.zh + 2, 4)), 0, self.zf_r).wait_recv()
 
     def x_copy(self, q, way):
         block = self.slot(self.x, mod(self.zh + q, 4))
-        return pltpu.make_async_remote_copy(
-            self.own if q == 0 else block, block, self.sent.at[1], self.x_r.at[q, way],
-            device_id=self.device(0, 1 - 2 * way), device_id_type=MESH)
+        return self.copy(self.own if q == 0 else block, block, 1, self.x_r.at[q, way], 0, 1 - 2 * way)
 
     def x_start(self, q):
         for way in range(2):
             self.x_copy(q, way).start()
 
-    def x_forward_copy(self, q, way):
-        block = self.part(self.slot(mod(self.x - (1 - 2 * way), 4), mod(self.zh + q, 4)), way)
-        return pltpu.make_async_remote_copy(
-            block, block, self.sent.at[2], self.xf_r.at[q],
-            device_id=self.device(0, 1 - 2 * way), device_id_type=MESH)
-
     def x_forward(self, q):
         for way in range(2):
             self.x_copy(q, way).wait_recv()
-            self.x_forward_copy(q, way).start()
+            block = self.part(mod(self.x - (1 - 2 * way), 4), mod(self.zh + q, 4), way)
+            self.copy(block, block, 2, self.xf_r.at[q], 0, 1 - 2 * way).start()
 
     def x_last(self, q):
-        block = self.slot(mod(self.x + 2, 4), mod(self.zh + q, 4))
-        self.whole(block, self.sent.at[2], self.xf_r.at[q]).wait_recv()
+        self.whole(self.slot(mod(self.x + 2, 4), mod(self.zh + q, 4)), 2, self.xf_r.at[q]).wait_recv()
 
     def drain(self):
-        for i, blocks in enumerate((self.ref.at[0, pl.ds(0, 3)], self.ref.at[pl.ds(0, 2)], self.ref.at[0])):
-            self.whole(blocks, self.sent.at[i], self.zf_r).wait_send()
+        rows = pl.ds(self.first, self.rows)
+        sent = (self.ref.at[0, pl.ds(0, 3), rows], self.ref.at[pl.ds(0, 2), :, rows], self.ref.at[0, :, rows])
+        for i, blocks in enumerate(sent):
+            self.whole(blocks, i, self.zf_r).wait_send()
+
+
+class RowGather(Gather):
+    first, rows = FIRST_Z, COLS - FIRST_Z
+
+    def x_copy(self, way):
+        return self.copy(self.own, self.slot(self.x, self.zh), 0, self.x_r.at[way], 0, 1 - 2 * way)
+
+    def x_start(self):
+        for way in range(2):
+            self.x_copy(way).start()
+
+    def x_forward(self):
+        for way in range(2):
+            self.x_copy(way).wait_recv()
+            block = self.part(mod(self.x - (1 - 2 * way), 4), self.zh, way)
+            self.copy(block, block, 0, self.xf_r, 0, 1 - 2 * way).start()
+
+    def x_last(self):
+        self.whole(self.slot(mod(self.x + 2, 4), self.zh), 0, self.xf_r).wait_recv()
+
+    def z_copy(self, way):
+        blocks = self.ref.at[self.zh, :, pl.ds(self.first, self.rows)]
+        return self.copy(blocks, blocks, 1, self.z_r.at[way], 1 - 2 * way, 0)
+
+    def z_forward(self):
+        size = self.rows // 2
+        for way in range(2):
+            self.z_copy(way).wait_recv()
+            blocks = self.ref.at[mod(self.zh - (1 - 2 * way), 4), :, pl.ds(self.first + way * size, size)]
+            self.copy(blocks, blocks, 1, self.zf_r, 1 - 2 * way, 0).start()
+
+    def z_last(self):
+        blocks = self.ref.at[mod(self.zh + 2, 4), :, pl.ds(self.first, self.rows)]
+        self.whole(blocks, 1, self.zf_r).wait_recv()
+
+    def drain(self):
+        rows = pl.ds(self.first, self.rows)
+        for i, blocks in enumerate((self.ref.at[0, pl.ds(0, 3), rows], self.ref.at[pl.ds(0, 3), :, rows])):
+            self.whole(blocks, i, self.zf_r).wait_send()
 
 
 def kernel(
@@ -110,6 +145,8 @@
     load_sem, tk_s, tk_r, tg_s, tg_r,
     u_s, uz_r, uzf_r, ux_r, uxf_r,
     d_s, dz_r, dzf_r, dx_r, dxf_r,
+    ru_s, ruz_r, ruzf_r, rux_r, ruxf_r,
+    rd_s, rdz_r, rdzf_r, rdx_r, rdxf_r,
     cs_s, cs_r, rs_s, rs_r, pair_s, pair_r, ag_s, ag_r, agp_r, ac_s, ac_r,
     mx_s, mx_r, mf_s, mf_r, mz_s, mz_r, out_sem,
 ):
@@ -183,13 +220,16 @@
 
     target_copy = remote(pair.at[core], pair.at[core], tg_s, tg_r, sibling)
 
-    up_gather = Gather(upb, COLS, up_ref, (u_s, uz_r, uzf_r, ux_r, uxf_r), zh, x, device)
-    down_gather = Gather(dnb, COLS, down_ref, (d_s, dz_r, dzf_r, dx_r, dxf_r), zh, x, device)
+    up_gather = Gather(upb, up_ref, (u_s, uz_r, uzf_r, ux_r, uxf_r), zh, x, device)
+    down_gather = Gather(dnb, down_ref, (d_s, dz_r, dzf_r, dx_r, dxf_r), zh, x, device)
+    up_other = RowGather(upb, up_ref, (ru_s, ruz_r, ruzf_r, rux_r, ruxf_r), zh, x, device)
+    down_other = RowGather(dnb, down_ref, (rd_s, rdz_r, rdzf_r, rdx_r, rdxf_r), zh, x, device)
 
     tk_copy(1, 0).start()
     for b in range(1, 4):
         tk_copy(0, b).start()
     up_gather.z_start()
+    up_other.x_start()
     up_gather.x_start(0)
     tk_pass(0, 0).start()
     target_copy.start()
@@ -198,18 +238,24 @@
     for b in range(1, 4):
         tk_copy(1, b).start()
     tk_pass(1, 0).start()
+    up_other.x_forward()
+    down_other.x_start()
     down_gather.x_start(0)
     up_gather.x_forward(0)
     up_gather.z_forward()
     up_gather.x_start(1)
     up_gather.x_start(3)
-    down_gather.z_start()
+    loads[0].wait()
+    up_other.x_last()
+    up_other.z_start()
+    down_other.x_forward()
     tk_wait(3, 0, 1).wait_recv()
     for b in range(1, 4):
         tk_pass(0, b).start()
-    down_gather.x_forward(0)
     up_gather.z_last()
     up_gather.x_start(2)
+    down_gather.z_start()
+    down_gather.x_forward(0)
     tk_wait(3, 0, 3).wait_recv()
     for b in range(1, 4):
         tk_pass(1, b).start()
@@ -223,28 +269,28 @@
         x_all[pl.ds(pl.multiple_of(c * 48, 48), 48), :] = jnp.concatenate(rows, axis=0).astype(bf16)
 
     up_gather.x_forward(3)
+    up_other.z_forward()
+
+    def joined(ref, row, first, count):
+        return jnp.concatenate([ref[row, first + i] for i in range(count)], axis=1)
+
+    def rows_dot(left, right):
+        return lax.dot_general(left, right, (((1,), (1,)), ((), ())), preferred_element_type=f32)
+
+    def wide_dot(acc, weight):
+        acc[...] = rows_dot(x_all[...], weight[...])
+
+    loads[2].wait()
+    wide_dot(gate_acc, w_ref)
+    up_gather.x_forward(2)
     down_gather.z_forward()
     down_gather.x_start(1)
     down_gather.x_start(3)
-
-    def joined(ref, row, first, count):
-        return jnp.concatenate([ref[row, first + i] for i in range(count)], axis=1)
-
-    def rows_dot(left, right):
-        return lax.dot_general(left, right, (((1,), (1,)), ((), ())), preferred_element_type=f32)
-
-    def wide_dot(acc, weight):
-        acc[...] = rows_dot(x_all[...], weight[...])
-
-    loads[2].wait()
-    wide_dot(gate_acc, w_ref)
-    up_gather.x_forward(2)
+    loads[1].wait()
+    down_other.x_last()
+    down_other.z_start()
     loads[3].wait()
     wide_dot(probe_acc, p_ref)
-    down_gather.z_last()
-    down_gather.x_start(2)
-    loads[0].wait()
-    loads[1].wait()
 
     def up_rows(q):
         row = mod(zh + q, 4)
@@ -252,9 +298,12 @@
 
     for q in (0, 1, 3):
         up_gather.x_last(q)
+    up_other.z_last()
     up_acc[...] = up_rows(0) + up_rows(1) + up_rows(3)
     up_gather.x_last(2)
     up_acc[...] += up_rows(2)
+    down_gather.z_last()
+    down_gather.x_start(2)
 
     @pl.loop(0, 8)
     def _(c):
@@ -272,6 +321,8 @@
         probe_acc[rows, :] = up_pre * slope_two * probe_pre
 
     target_copy.wait_recv()
+    down_gather.x_forward(1)
+    down_other.z_forward()
 
     order = (0, 1, 3, 2)
 
@@ -410,26 +461,37 @@
 
     def ready(s):
         down_gather.x_last(order[s])
-
-    def passed_on(step):
-        if step < 3:
-            down_gather.x_forward(order[step + 1])
-
-    for step in range(8):
-        if step < 4:
-            ready(step)
-            forward(step, 0)
-            passed_on(step)
-        if 0 <= step - 1 < 4:
-            scatter(step - 1, 0)
-        if step in (4, 5):
-            turn(step - 4)
-        if 0 <= step - 2 < 4:
-            reduce(step - 2, 0)
-        if 0 <= step - 3 < 4:
-            across(step - 3, 0)
-        if 0 <= step - 4 < 4:
-            backward(step - 4, 0, grad_acc)
+        if s == 3:
+            down_other.z_last()
+
+    def sums(s):
+        ready(s)
+        forward(s, 0)
+
+    sums(0)
+    down_gather.x_forward(3)
+    sums(1)
+    scatter(0, 0)
+    scatter(1, 0)
+    down_gather.x_forward(2)
+    sums(2)
+    reduce(0, 0)
+    scatter(2, 0)
+    sums(3)
+    reduce(1, 0)
+    scatter(3, 0)
+    across(0, 0)
+    turn(0)
+    reduce(2, 0)
+    backward(0, 0, grad_acc)
+    across(1, 0)
+    turn(1)
+    reduce(3, 0)
+    backward(1, 0, grad_acc)
+    across(2, 0)
+    backward(2, 0, grad_acc)
+    across(3, 0)
+    backward(3, 0, grad_acc)
 
     loads[4].wait()
     tang_acc[...] = jnp.zeros_like(tang_acc)
@@ -615,6 +677,8 @@
         out_copy(out_t, 0, slot).wait()
     up_gather.drain()
     down_gather.drain()
+    up_other.drain()
+    down_other.drain()
     target_copy.wait_send()
 
     tk_wait(7, 0, 0).wait_send()
@@ -643,6 +707,7 @@
     wide = pltpu.VMEM((TOK, COLS), f32)
     turned = pltpu.VMEM((COLS, TOK), f32)
     mixed = pltpu.VMEM((2 * NC, COLS, CH), bf16)
+    other_sems = [dma((2,)), dma((2,)), dma, dma((2,)), dma]
     gather_sems = [dma((3,)), dma((2,)), dma, dma((4, 2)), dma((4,))]
     mixed_weights, mixed_tracker = pl.pallas_call(
         kernel,
@@ -675,7 +740,7 @@
             pltpu.VMEM((4, COLS, CH), f32),
             pltpu.VMEM((2, COLS, CH), bf16),
             dma((7,)), dma((2,)), dma((4,)), dma, dma,
-            *gather_sems, *gather_sems,
+            *gather_sems, *gather_sems, *other_sems, *other_sems,
             dma, dma((2, 4)), dma((2,)), dma((2, 4)), dma, dma((4,)),
             dma((2,)), dma((2, 4)), dma((4,)), dma, dma((2, 4)),
             dma((RING, 2)), dma((RING, 2)), dma((RING, 2)), dma((RING, 2)),

time: 254 us -> 250 us (0.984)
  Pallas kernels: 248 us -> 245 us
    pallas_call x1, Pallas kernels: 248 us -> 245 us  [local(): pl.pallas_call(kernel, out_shape=(weight, weight), in_specs=[vmem, vmem,...]
where the time goes in v4:
time: 250 us
  Pallas kernels  245 us (98%)
  local copies, waits for them, and re-layouts  4.3 us (2%)
    pallas_call x1, Pallas kernels, local(): pl.pallas_call(kernel, out_shape=(weight, weight), in_specs=[vmem, vmem,...  245 us

profile of v4, /device:TPU:16, one launch (start us, length us, event | category | flops | bytes accessed | tf_op | source)
XLA Modules:
  0.0 249.5 jit_solution(12669187500770802265)
XLA Ops:
  0.6 244.6 %step_and_mix.1 = (bf16[448,2048]{1,0:T(8,128)(2,1)}, bf16[448,2048]{1,0:T(8,128)(2,1)}) custom-call(bf16[24,2048]{1,0:T(8,128)(2,1)} %bitcast.26, bf16[24,2048]{1,0:T(8,128)(2,1)} %bitcast.27, bf16[448,2048]{1,0:T(8,128)(2,1)} %bitcast.22, bf16[448,2048]{1,0:T(8,128)(2,1)} %bitcast.23, bf16[448,2048]{1,0:T(8,128)(2,1)} %bitcast.24, ...), custom_call_target="tpu_custom_call" | custom-call | tf_op jit(solution)/shard_map/step_and_mix/pallas_call | solution.py:712
  245.2 0.0 copy-start
  245.2 3.1 %copy.13 = bf16[1,2048,448]{1,2,0:T(8,128)(2,1)} copy(bf16[1,2048,448]{1,2,0:T(8,128)(2,1)} %bitcast.21) | data formatting | bytes 3670016
  248.3 0.0 copy-done
  248.3 1.2 copy.14
Async XLA Ops:
  245.2 3.1 %copy-start = (bf16[448,2048]{1,0:T(8,128)(2,1)S(1)}, bf16[448,2048]{1,0:T(8,128)(2,1)}, u32[]{:S(2)}) copy-start(bf16[448,2048]{1,0:T(8,128)(2,1)} %get-tuple-element.5) | copy-start | bytes 5505028

commit v5 on v4

--- a/solution.py
+++ b/solution.py
@@ -695,6 +695,29 @@
         for way in range(2):
             mx_copy(g, way).wait_send()
             mz_copy(g, way).wait_send()
+
+
+PIECES = 4
+
+
+def hand_on(a_ref, b_ref, a_out, b_out, held, in_sem, out_sem):
+    size = COLS // PIECES
+    pairs = ((a_ref, a_out), (b_ref, b_out))
+
+    def copies(i, c):
+        rows = pl.ds(c * size, size)
+        inward = pltpu.make_async_copy(pairs[i][0].at[rows], held.at[i, rows], in_sem.at[i, c])
+        outward = pltpu.make_async_copy(held.at[i, rows], pairs[i][1].at[rows], out_sem.at[i, c])
+        return inward, outward
+
+    every = [copies(i, c) for i in range(2) for c in range(PIECES)]
+    for inward, _ in every:
+        inward.start()
+    for inward, outward in every:
+        inward.wait()
+        outward.start()
+    for _, outward in every:
+        outward.wait()
 
 
 def local(
@@ -754,7 +777,19 @@
         tokens[0], targets[0], gate_weight[0].T, probes[0].T, tracker[0].T, up_weight.T, down_weight,
         neighbours.T, numerators.T,
     )
-    return (mixed_weights.T[None], mixed_tracker.T[None])
+    handed = pl.pallas_call(
+        hand_on,
+        out_shape=(weight, weight),
+        in_specs=[hbm, hbm],
+        out_specs=(hbm, hbm),
+        scratch_shapes=[
+            pltpu.VMEM((2, COLS, D), bf16),
+            dma((2, PIECES)), dma((2, PIECES)),
+        ],
+        compiler_params=pltpu.CompilerParams(vmem_limit_bytes=60 << 20),
+        name="hand_on",
+    )(mixed_weights, mixed_tracker)
+    return (handed[0].T[None], handed[1].T[None])
 
 
 def solution(mesh):

time: 250 us -> 248 us (level)
  local copies, waits for them, and re-layouts: 4.3 us -> 0 us
  Pallas kernels: 245 us -> 248 us
    unnamed x4 -> x0, local copies, waits for them, and re-layouts: 4.3 us -> none
    pallas_call x0 -> x1, Pallas kernels: none -> 3.06 us  [local(): pl.pallas_call(hand_on, out_shape=(weight, weight), in_specs=[hbm, hbm],...]
where the time goes in v5:
time: 248 us
  Pallas kernels  248 us (100%)
    pallas_call x1, Pallas kernels, local(): pl.pallas_call(kernel, out_shape=(weight, weight), in_specs=[vmem, vmem,...  245 us

profile of v5, /device:TPU:16, one launch (start us, length us, event | category | flops | bytes accessed | tf_op | source)
XLA Modules:
  0.0 248.3 jit_solution(16881940311467600648)
XLA Ops:
  0.6 244.6 %step_and_mix.1 = (bf16[448,2048]{1,0:T(8,128)(2,1)}, bf16[448,2048]{1,0:T(8,128)(2,1)}) custom-call(bf16[24,2048]{1,0:T(8,128)(2,1)} %bitcast.24, bf16[24,2048]{1,0:T(8,128)(2,1)} %bitcast.25, bf16[448,2048]{1,0:T(8,128)(2,1)} %bitcast.20, bf16[448,2048]{1,0:T(8,128)(2,1)} %bitcast.21, bf16[448,2048]{1,0:T(8,128)(2,1)} %bitcast.22, ...), custom_call_target="tpu_custom_call" | custom-call | tf_op jit(solution)/shard_map/step_and_mix/pallas_call | solution.py:735
  245.2 3.1 %hand_on.1 = (bf16[448,2048]{1,0:T(8,128)(2,1)}, bf16[448,2048]{1,0:T(8,128)(2,1)}) custom-call(bf16[448,2048]{1,0:T(8,128)(2,1)} %get-tuple-element.6.a_ref, bf16[448,2048]{1,0:T(8,128)(2,1)} %get-tuple-element.7.b_ref), custom_call_target="tpu_custom_call" | custom-call | tf_op jit(solution)/shard_map/hand_on/pallas_call | solution.py:780

commit v6 on v5

--- a/solution.py
+++ b/solution.py
@@ -629,8 +629,8 @@
     produce(0, 0)
     x_send(0)
     produce(0, 1)
+    x_pass(0)
     x_send(1)
-    x_pass(0)
 
     @pl.loop(0, 2 * NC + 2)
     def _(g):

time: 248 us -> 250 us (level); the launches traced: 248 us -> 247 us
  no operation moved by 1% of the time
where the time goes in v6:
time: 250 us; the launch traced here: 247 us
  Pallas kernels  246 us (98%)
    pallas_call x1, Pallas kernels, local(): pl.pallas_call(kernel, out_shape=(weight, weight), in_specs=[vmem, vmem,...  243 us

profile of v6, /device:TPU:16, one launch (start us, length us, event | category | flops | bytes accessed | tf_op | source)
XLA Modules:
  0.0 246.8 jit_solution(16655313975269053614)
XLA Ops:
  0.6 243.1 %step_and_mix.1 = (bf16[448,2048]{1,0:T(8,128)(2,1)}, bf16[448,2048]{1,0:T(8,128)(2,1)}) custom-call(bf16[24,2048]{1,0:T(8,128)(2,1)} %bitcast.24, bf16[24,2048]{1,0:T(8,128)(2,1)} %bitcast.25, bf16[448,2048]{1,0:T(8,128)(2,1)} %bitcast.20, bf16[448,2048]{1,0:T(8,128)(2,1)} %bitcast.21, bf16[448,2048]{1,0:T(8,128)(2,1)} %bitcast.22, ...), custom_call_target="tpu_custom_call" | custom-call | tf_op jit(solution)/shard_map/step_and_mix/pallas_call | solution.py:735
  243.7 3.1 %hand_on.1 = (bf16[448,2048]{1,0:T(8,128)(2,1)}, bf16[448,2048]{1,0:T(8,128)(2,1)}) custom-call(bf16[448,2048]{1,0:T(8,128)(2,1)} %get-tuple-element.6.a_ref, bf16[448,2048]{1,0:T(8,128)(2,1)} %get-tuple-element.7.b_ref), custom_call_target="tpu_custom_call" | custom-call | tf_op jit(solution)/shard_map/hand_on/pallas_call | solution.py:780
